TPU v7x, 32 devices: a whole 2x2x4 slice. The times are simulated.
32 devices in a mesh: dp: 8 (over z, y), expert: 4 (over x, core).
Axes of the slice: x: 2, y: 2, z: 4, core: 2. Of those that a mesh axis runs over, the one named last changes fastest.
Arguments:
- frames: bfloat16 [4096, 1024], P(('dp', 'expert')), may hold values from -6 to 6
- expert_ids: int32 [4096, 2], P(('dp', 'expert')), may hold values from 0 to 3, all different within a row; in each aligned block of 128 rows (0 to 127, 128 to 255, ...) at most 128 rows name the same one
- gate_weights: float32 [4096, 2], P(('dp', 'expert')), may hold values from 0.2 to 1
- cotangent: bfloat16 [4096, 1024], P(('dp', 'expert')), may hold values from -6 to 6
- w_in: bfloat16 [4, 1024, 2048], P('expert'), may hold values from -0.1875 to 0.1875
- w_out: bfloat16 [4, 2048, 1024], P('expert'), may hold values from -0.125 to 0.125
Outputs:
- mixed: bfloat16 [4096, 1024], P(('dp', 'expert'))
- grad_frames: bfloat16 [4096, 1024], P(('dp', 'expert'))
- grad_w_in: float32 [4, 1024, 2048], P('expert', 'dp')
- grad_w_out: float32 [4, 2048, 1024], P('expert', 'dp')
Inputs may be any that keep to these rules, and one draw needn't show every extreme that they name: `expert_ids`: the two experts of a frame differ. Among the 128 frames of one device (aligned blocks of rows), no expert is named by more than 128 of them, and in some block one expert is named by exactly 128.
All inputs are finite; a program needn't handle non-finite values.
Results may differ from a plain program's by a relative error of at most 0.015.
Values may be sent and summed in bfloat16 or wider, within the bound.
A program may use at most 128 MiB of HBM per device.

v0:
```python
import jax
import jax.numpy as jnp
from jax import lax
from jax.sharding import PartitionSpec as P


def normalize(values):
    center = values - jnp.mean(values, axis=-1, keepdims=True)
    inverse = lax.rsqrt(jnp.mean(center * center, axis=-1, keepdims=True) + 1e-05)
    return (center * inverse, inverse)


def slot_index(id_block, experts, capacity):
    flat_ids = id_block.reshape(-1)
    one_hot = (flat_ids[:, None] == jnp.arange(experts, dtype=jnp.int32)[None, :]).astype(jnp.int32)
    earlier = jnp.cumsum(one_hot, axis=0) - one_hot
    return flat_ids * capacity + jnp.sum(earlier * one_hot, axis=1)


def route_rows(buffer):
    result = lax.all_to_all(buffer, "expert", split_axis=0, concat_axis=0, tiled=True)
    return result


def per_device(frames, expert_ids, gate_weights, cotangent, w_in, w_out):
    tok_rows = frames.shape[0]
    width = frames.shape[1]
    peers = lax.axis_size("expert")
    local_experts = w_in.shape[0]
    experts = peers * local_experts
    capacity = 4 * tok_rows // experts
    values = frames.astype(jnp.float32)
    standardized, inverse = normalize(values)
    normed = standardized.astype(jnp.bfloat16)
    target = slot_index(expert_ids, experts, capacity)

    def place(rows):
        filled = jnp.zeros((experts * capacity, width), jnp.bfloat16).at[target].set(rows)
        return filled.reshape(peers, local_experts * capacity, width)

    def arrive(rows):
        return route_rows(place(rows)).reshape(peers, local_experts, capacity, width)

    def depart(rows):
        return route_rows(rows.reshape(peers, local_experts * capacity, width)).reshape(
            experts * capacity, width
        )

    received = arrive(jnp.repeat(normed, 2, axis=0))
    pre_act = jnp.einsum("secd,edh->sech", received, w_in, preferred_element_type=jnp.float32)
    sigma = jax.nn.sigmoid(pre_act)
    hidden = (pre_act * sigma).astype(jnp.bfloat16)
    expert_out = jnp.einsum(
        "sech,ehd->secd", hidden, w_out, preferred_element_type=jnp.float32
    ).astype(jnp.bfloat16)
    returned = depart(expert_out)
    flat_gates = gate_weights.reshape(-1, 1)
    picked = jnp.take(returned, target, axis=0).astype(jnp.float32) * flat_gates
    mixed = (values + 0.5 * picked.reshape(tok_rows, 2, width).sum(axis=1)).astype(jnp.bfloat16)
    upstream = cotangent.astype(jnp.float32)
    grad_rows = (jnp.repeat(upstream, 2, axis=0) * (0.5 * flat_gates)).astype(jnp.bfloat16)
    grad_recv = arrive(grad_rows)
    grad_hidden = jnp.einsum("secd,ehd->sech", grad_recv, w_out, preferred_element_type=jnp.float32)
    grad_pre = (grad_hidden * (sigma + pre_act * sigma * (1.0 - sigma))).astype(jnp.bfloat16)
    grad_back = jnp.einsum(
        "sech,edh->secd", grad_pre, w_in, preferred_element_type=jnp.float32
    ).astype(jnp.bfloat16)
    back_rows = depart(grad_back)
    grad_normed = (
        jnp.take(back_rows, target, axis=0)
        .astype(jnp.float32)
        .reshape(tok_rows, 2, width)
        .sum(axis=1)
    )
    centered = grad_normed - jnp.mean(grad_normed, axis=-1, keepdims=True)
    along = standardized * jnp.mean(grad_normed * standardized, axis=-1, keepdims=True)
    grad_frames = (upstream + inverse * (centered - along)).astype(jnp.bfloat16)
    piece = hidden
    grad_w_out = (
        lax.psum_scatter(
            jnp.einsum(
                "sech,secd->hed", piece, grad_recv, preferred_element_type=jnp.float32
            ).astype(jnp.bfloat16),
            "dp",
            scatter_dimension=0,
            tiled=True,
        )
        .astype(jnp.float32)
        .transpose(1, 0, 2)
    )
    piece = received
    grad_w_in = (
        lax.psum_scatter(
            jnp.einsum(
                "secd,sech->deh", piece, grad_pre, preferred_element_type=jnp.float32
            ).astype(jnp.bfloat16),
            "dp",
            scatter_dimension=0,
            tiled=True,
        )
        .astype(jnp.float32)
        .transpose(1, 0, 2)
    )
    return (mixed, grad_frames, grad_w_in, grad_w_out)


def solution(mesh):
    return jax.shard_map(
        per_device,
        mesh=mesh,
        in_specs=(
            P(("dp", "expert"), None),
            P(("dp", "expert"), None),
            P(("dp", "expert"), None),
            P(("dp", "expert"), None),
            P("expert", None, None),
            P("expert", None, None),
        ),
        out_specs=(
            P(("dp", "expert"), None),
            P(("dp", "expert"), None),
            P("expert", "dp", None),
            P("expert", "dp", None),
        ),
        check_vma=False,
    )
```

profile of v0, /device:TPU:0, one launch (start us, length us, event | category | flops | bytes accessed | tf_op | source)
XLA Modules:
  0.0 251.8 jit_solution(2954826936552145549)
XLA Ops:
  7.2 0.7 broadcast_multiply_fusion.1
  7.9 0.8 copy.26
  8.7 0.1 eq.25
  8.8 0.1 eq.29
  9.0 1.1 convert_reduce_fusion
  10.1 1.2 fusion.42
  11.2 0.1 copy.30
  11.3 0.1 mul.98
  11.5 1.2 reduce-window.6
  12.7 0.1 slice.12
  12.8 0.1 copy.28
  13.0 0.1 copy.29
  13.1 0.1 add_bitcast_fusion
  13.1 1.2 fusion.34
  14.3 0.3 broadcast_in_dim.13
  14.6 0.2 reshape.186
  14.8 2.6 %scatter_custom_fusion = bf16[512,1024]{1,0:T(8,128)(2,1)} fusion(s32[256]{0:T(256)S(1)} %bitcast.134, bf16[256,1024]{1,0:T(8,128)(2,1)S(1)} %reshape.186, bf16[]{:T(256)} %constant.17.clone.1), kind=kCustom, calls=%fused_computation.52 | custom fusion | bytes 1048578 | tf_op jit(solution)/shard_map/scatter | solution.py:38
  17.5 4.2 %all-to-all-start = ((bf16[4,128,1024]{2,1,0:T(8,128)(2,1)}), bf16[4,128,1024]{2,1,0:T(8,128)(2,1)S(1)}, u32[]{:S(2)}, u32[]{:S(2)}) async-start(bf16[4,128,1024]{2,1,0:T(8,128)(2,1)} %bitcast.4), calls=%async_computation | async-start | bytes 2097152 | tf_op jit(solution)/shard_map/all_to_all | solution.py:21
  21.7 0.0 copy-done.2
  21.7 0.1 copy.31
  21.8 0.1 mul.106
  21.9 0.3 broadcast_in_dim.14
  22.2 0.7 reshape.159
  23.0 2.7 %scatter_custom_fusion.1 = bf16[512,1024]{1,0:T(8,128)(2,1)} fusion(s32[256]{0:T(256)S(1)} %bitcast.135, f32[256,1024]{1,0:T(8,128)S(1)} %reshape.159, f32[256]{0:T(256)S(1)} %broadcast_multiply_fusion, bf16[]{:T(256)} %constant.17.clone.1), kind=kCustom, calls=%fused_computation.46 | custom fusion | flops 524288 | bytes 2098178 | tf_op jit(solution)/shard_map/scatter | solution.py:38
  25.7 10.5 %all-to-all-done = bf16[4,128,1024]{2,1,0:T(8,128)(2,1)S(1)} async-done(((bf16[4,128,1024]{2,1,0:T(8,128)(2,1)}), bf16[4,128,1024]{2,1,0:T(8,128)(2,1)S(1)}, u32[]{:S(2)}, u32[]{:S(2)}) %all-to-all-start) | async-done | bytes 1048608 | tf_op jit(solution)/shard_map/all_to_all | solution.py:21
  36.1 3.5 %all-to-all-start.2 = ((bf16[4,128,1024]{2,1,0:T(8,128)(2,1)}), bf16[4,128,1024]{2,1,0:T(8,128)(2,1)S(1)}, u32[]{:S(2)}, u32[]{:S(2)}) async-start(bf16[4,128,1024]{2,1,0:T(8,128)(2,1)} %bitcast.16), calls=%async_computation.2 | async-start | bytes 2097152 | tf_op jit(solution)/shard_map/all_to_all | solution.py:21
  39.7 0.0 reduce-scatter.5.cloned.1.call-start
  39.7 6.5 %fusion.10 = f32[4,128,2048]{2,1,0:T(8,128)} fusion(bf16[4,128,1024]{2,1,0:T(8,128)(2,1)S(1)} %all-to-all-done, bf16[1,1024,2048]{2,1,0:T(8,128)(2,1)} %param.12), kind=kOutput, calls=%fused_computation.19 | convolution fusion | flops 2147483648 | bytes 9437184 | tf_op jit(solution)/shard_map/secd,edh->sech/dot_general | solution.py:50
  46.2 7.9 %all-to-all-done.2 = bf16[4,128,1024]{2,1,0:T(8,128)(2,1)S(1)} async-done(((bf16[4,128,1024]{2,1,0:T(8,128)(2,1)}), bf16[4,128,1024]{2,1,0:T(8,128)(2,1)S(1)}, u32[]{:S(2)}, u32[]{:S(2)}) %all-to-all-start.2) | async-done | bytes 1048608 | tf_op jit(solution)/shard_map/all_to_all | solution.py:21
  54.1 6.6 %fusion.13 = bf16[2048,1,1024]{0,2,1:T(8,128)(2,1)} fusion(bf16[4,128,1024]{2,1,0:T(8,128)(2,1)S(1)} %all-to-all-done.2, f32[4,128,2048]{2,1,0:T(8,128)} %fusion.10), kind=kOutput, calls=%fused_computation.22 | convolution fusion | flops 2154823680 | bytes 9437184 | tf_op jit(solution)/shard_map/sech,secd->hed/dot_general | solution.py:81
  60.7 0.0 reduce-scatter.5.cloned.1.call-update
  60.7 0.2 reduce-scatter.7.cloned.1.call-start
  60.9 6.4 %fusion.17 = bf16[4,128,2048]{2,1,0:T(8,128)(2,1)S(1)} fusion(f32[4,128,2048]{2,1,0:T(8,128)} %fusion.10, bf16[4,128,1024]{2,1,0:T(8,128)(2,1)S(1)} %all-to-all-done.2, bf16[1,2048,1024]{2,1,0:T(8,128)(2,1)} %param.13), kind=kOutput, calls=%fused_computation.24 | convolution fusion | flops 2156920832 | bytes 11534336 | tf_op jit(solution)/shard_map/secd,ehd->sech/dot_general | solution.py:63
  67.4 1.3 copy-done.3
  68.7 4.4 %fusion.12 = bf16[1024,2048]{0,1:T(8,128)(2,1)} fusion(bf16[4,128,2048]{2,1,0:T(8,128)(2,1)S(1)} %fusion.17, bf16[4,128,1024]{2,1,0:T(8,128)(2,1)S(1)} %all-to-all-done), kind=kOutput, calls=%fused_computation.21 | convolution fusion | flops 2149580800 | bytes 7340032 | tf_op jit(solution)/shard_map/secd,sech->deh/dot_general | solution.py:94
  73.1 6.5 %copy.40 = bf16[1024,2048]{1,0:T(8,128)(2,1)} copy(bf16[1024,2048]{0,1:T(8,128)(2,1)} %fusion.12) | data formatting | bytes 8388608
  79.6 0.0 reduce-scatter.7.cloned.1.call-update
  79.6 0.0 copy-start.4
  79.6 7.0 %fusion.25 = bf16[4,128,1024]{2,1,0:T(8,128)(2,1)} fusion(bf16[1,2048,1024]{2,1,0:T(8,128)(2,1)} %param.13, f32[4,128,2048]{2,1,0:T(8,128)} %fusion.10), kind=kOutput, calls=%fused_computation.28 | convolution fusion | flops 2153250816 | bytes 9437184 | tf_op jit(solution)/shard_map/sech,ehd->secd/dot_general | solution.py:53
  86.6 3.5 %all-to-all-start.1 = ((bf16[4,128,1024]{2,1,0:T(8,128)(2,1)}), bf16[4,128,1024]{2,1,0:T(8,128)(2,1)S(1)}, u32[]{:S(2)}, u32[]{:S(2)}) async-start(bf16[4,128,1024]{2,1,0:T(8,128)(2,1)} %fusion.25), calls=%async_computation.1 | async-start | bytes 2097152 | tf_op jit(solution)/shard_map/all_to_all | solution.py:21
  90.2 5.5 %fusion.22 = bf16[4,128,1024]{2,1,0:T(8,128)(2,1)} fusion(bf16[4,128,2048]{2,1,0:T(8,128)(2,1)S(1)} %copy-done.4, bf16[1,1024,2048]{2,1,0:T(8,128)(2,1)} %param.12), kind=kOutput, calls=%fused_computation.27 | convolution fusion | flops 2148007936 | bytes 7340032 | tf_op jit(solution)/shard_map/sech,edh->secd/dot_general | solution.py:65
  95.7 8.9 %all-to-all-done.1 = bf16[4,128,1024]{2,1,0:T(8,128)(2,1)S(1)} async-done(((bf16[4,128,1024]{2,1,0:T(8,128)(2,1)}), bf16[4,128,1024]{2,1,0:T(8,128)(2,1)S(1)}, u32[]{:S(2)}, u32[]{:S(2)}) %all-to-all-start.1) | async-done | bytes 1048608 | tf_op jit(solution)/shard_map/all_to_all | solution.py:21
  104.6 3.7 %all-to-all-start.3 = ((bf16[4,128,1024]{2,1,0:T(8,128)(2,1)}), bf16[4,128,1024]{2,1,0:T(8,128)(2,1)S(1)}, u32[]{:S(2)}, u32[]{:S(2)}) async-start(bf16[4,128,1024]{2,1,0:T(8,128)(2,1)} %fusion.22), calls=%async_computation.3 | async-start | bytes 2097152 | tf_op jit(solution)/shard_map/all_to_all | solution.py:21
  108.4 1.2 gather_fusion
  109.5 13.0 %all-to-all-done.3 = bf16[4,128,1024]{2,1,0:T(8,128)(2,1)S(1)} async-done(((bf16[4,128,1024]{2,1,0:T(8,128)(2,1)}), bf16[4,128,1024]{2,1,0:T(8,128)(2,1)S(1)}, u32[]{:S(2)}, u32[]{:S(2)}) %all-to-all-start.3) | async-done | bytes 1048608 | tf_op jit(solution)/shard_map/all_to_all | solution.py:21
  122.5 1.2 gather_fusion.1
  123.7 0.3 fusion.54
  124.0 0.1 reduce_sum.79
  124.2 0.0 copy-start
  124.2 1.1 select_convert_fusion
  125.3 1.8 reshape.163
  127.1 0.1 reduce_sum.80
  127.3 1.2 reduce_sum.77
  128.5 0.6 reshape.158
  129.1 1.2 reduce_sum.76
  130.4 0.2 fusion.37
  130.6 1.0 fusion.41
  131.6 18.8 %reduce-scatter.5.cloned.1.call-done = bf16[256,1,1024]{0,2,1:T(8,128)(2,1)} async-done(((bf16[2048,1,1024]{0,2,1:T(8,128)(2,1)}), bf16[256,1,1024]{0,2,1:T(8,128)(2,1)}) %reduce-scatter.5.cloned.1.call-update) | async-done | bytes 524304 | tf_op jit(solution)/shard_map/reduce_scatter | solution.py:80
  150.4 1.1 bitcast_convert_fusion.3
  151.5 1.3 copy.35
  152.8 89.5 %reduce-scatter.7.cloned.1.call-done = bf16[128,2048]{1,0:T(8,128)(2,1)} async-done(((bf16[1024,2048]{1,0:T(8,128)(2,1)}), bf16[128,2048]{1,0:T(8,128)(2,1)}) %reduce-scatter.7.cloned.1.call-update) | async-done | bytes 524304
  242.3 1.3 copy.41
  243.6 0.1 bitcast_convert_fusion.2
  243.7 1.3 copy.34
  (17 shorter events, 0.1 us)
Async XLA Ops:
  7.2 14.5 %copy-start.2 = (f32[128,2]{0,1:T(2,128)S(1)}, f32[128,2]{0,1:T(2,128)}, u32[]{:S(2)}) copy-start(f32[128,2]{0,1:T(2,128)} %param.10) | copy-start | bytes 3076
  7.2 14.7 %copy-start.1 = (bf16[128,1024]{1,0:T(8,128)(2,1)S(1)}, bf16[128,1024]{1,0:T(8,128)(2,1)}, u32[]{:S(2)}) copy-start(bf16[128,1024]{1,0:T(8,128)(2,1)} %param.11) | copy-start | bytes 786436
  17.5 18.7 %all-to-all-start = ((bf16[4,128,1024]{2,1,0:T(8,128)(2,1)}), bf16[4,128,1024]{2,1,0:T(8,128)(2,1)S(1)}, u32[]{:S(2)}, u32[]{:S(2)}) async-start(bf16[4,128,1024]{2,1,0:T(8,128)(2,1)} %bitcast.4), calls=%async_computation | async-start | bytes 2097152 | tf_op jit(solution)/shard_map/all_to_all | solution.py:21
  36.1 18.0 %all-to-all-start.2 = ((bf16[4,128,1024]{2,1,0:T(8,128)(2,1)}), bf16[4,128,1024]{2,1,0:T(8,128)(2,1)S(1)}, u32[]{:S(2)}, u32[]{:S(2)}) async-start(bf16[4,128,1024]{2,1,0:T(8,128)(2,1)} %bitcast.16), calls=%async_computation.2 | async-start | bytes 2097152 | tf_op jit(solution)/shard_map/all_to_all | solution.py:21
  39.7 110.8 %reduce-scatter.5.cloned.1.call-start = ((), (), s32[]{:S(2)}) async-start(), calls=%async_computation.6 | async-start | bytes 4718592 | tf_op jit(solution)/shard_map/reduce_scatter | solution.py:80
  60.7 181.6 %reduce-scatter.7.cloned.1.call-start = ((), (), s32[]{:S(2)}) async-start(), calls=%async_computation.7 | async-start | bytes 4718592
  67.4 1.4 copy-start.3
  79.6 10.6 %copy-start.4 = (bf16[4,128,2048]{2,1,0:T(8,128)(2,1)S(1)}, bf16[4,128,2048]{2,1,0:T(8,128)(2,1)}, u32[]{:S(2)}) copy-start(bf16[4,128,2048]{2,1,0:T(8,128)(2,1)} %copy-done.3) | copy-start | bytes 6291460
  86.6 18.0 %all-to-all-start.1 = ((bf16[4,128,1024]{2,1,0:T(8,128)(2,1)}), bf16[4,128,1024]{2,1,0:T(8,128)(2,1)S(1)}, u32[]{:S(2)}, u32[]{:S(2)}) async-start(bf16[4,128,1024]{2,1,0:T(8,128)(2,1)} %fusion.25), calls=%async_computation.1 | async-start | bytes 2097152 | tf_op jit(solution)/shard_map/all_to_all | solution.py:21
  104.6 18.0 %all-to-all-start.3 = ((bf16[4,128,1024]{2,1,0:T(8,128)(2,1)}), bf16[4,128,1024]{2,1,0:T(8,128)(2,1)S(1)}, u32[]{:S(2)}, u32[]{:S(2)}) async-start(bf16[4,128,1024]{2,1,0:T(8,128)(2,1)} %fusion.22), calls=%async_computation.3 | async-start | bytes 2097152 | tf_op jit(solution)/shard_map/all_to_all | solution.py:21
  124.2 6.2 %copy-start = (bf16[128,1024]{1,0:T(8,128)(2,1)S(1)}, bf16[128,1024]{1,0:T(8,128)(2,1)}, u32[]{:S(2)}) copy-start(bf16[128,1024]{1,0:T(8,128)(2,1)} %param.8) | copy-start | bytes 786436
Sparse Core Ops, SparseCore 0:
  60.8 89.5 reduce-scatter.4
  154.5 87.7 reduce-scatter.6
where the time goes:
time: 253 us; the launch traced here: 252 us
  waiting for transfers between devices  149 us (59%)
  matrix products  36.5 us (14%)
  local copies, waits for them, and re-layouts  22.6 us (9%)
  starting transfers between devices  15.2 us (6%)
  other arithmetic  14.7 us (6%)
  between operations  14.3 us (6%)
    unnamed x3, waiting for transfers between devices  89.5 us
    all_to_all x4, waiting for transfers between devices, route_rows(): lax.all_to_all(buffer, 'expert', split_axis=0, concat_axis=0, tiled=True)  40.2 us
    reduce_scatter x1, waiting for transfers between devices, per_device(): lax.psum_scatter(jnp.einsum('sech,secd->hed', piece, grad_recv, preferred...  18.8 us
    all_to_all x4, starting transfers between devices, route_rows(): lax.all_to_all(buffer, 'expert', split_axis=0, concat_axis=0, tiled=True)  15 us
    unnamed x16, local copies, waits for them, and re-layouts  12.6 us
    dot_general x1, matrix products, per_device(): jnp.einsum('sech,ehd->secd', hidden, w_out, preferred_element_type=jnp.fl...  7.03 us
    dot_general x1, matrix products, per_device(): jnp.einsum('sech,secd->hed', piece, grad_recv, preferred_element_type=jnp...  6.6 us
    dot_general x1, matrix products, per_device(): jnp.einsum('secd,edh->sech', received, w_in, preferred_element_type=jnp.f...  6.5 us
  transfers between devices with their start and end apart: 6, of which 6 were waited for; matrix products, arithmetic and copies ran while one was open for 21% of the time, Pallas kernels for 0%

commit v1 on v0

--- a/solution.py
+++ b/solution.py
@@ -1,6 +1,10 @@
+import functools
+
 import jax
 import jax.numpy as jnp
 from jax import lax
+from jax.experimental import pallas as pl
+from jax.experimental.pallas import tpu as pltpu
 from jax.sharding import PartitionSpec as P
 
 
@@ -104,9 +108,318 @@
     return (mixed, grad_frames, grad_w_in, grad_w_out)
 
 
+MESH = pl.DeviceIdType.MESH
+
+
+def standardize(values):
+    center = values - jnp.mean(values, axis=-1, keepdims=True)
+    inverse = lax.rsqrt(jnp.mean(center * center, axis=-1, keepdims=True) + 1e-05)
+    return center * inverse, inverse
+
+
+def dot(a, b, contract_a, contract_b):
+    return lax.dot_general(
+        a, b, (((contract_a,), (contract_b,)), ((), ())), preferred_element_type=jnp.float32
+    )
+
+
+def layer_kernel(
+    tile,
+    frames, cot, gates, w_in, w_out,
+    mixed, grad_frames, grad_w_in, grad_w_out,
+    nrm, cots, gts, gcol, grow, hid, gpre, wi, wo, pm, pg, rm, rg,
+    syo, syi, ryo, ryi, owo, owi, szo, szi, rzo, rzi, sl, rl,
+    w_sem, ag_send, ag_recv, rs_send, rs_recv, dw_send, dw_recv,
+):
+    tok, width = frames.shape
+    rows = nrm.shape[0]
+    half = wi.shape[1]
+    chunk = half // 2
+    h_own = grad_w_out.shape[1]
+    d_own = grad_w_in.shape[1]
+    pairs = rows // (2 * tok)
+    d, e = lax.axis_index("dp"), lax.axis_index("expert")
+    zhi, rest = lax.div(d, 4), lax.rem(d, 4)
+    zlo, y = lax.div(rest, 2), lax.rem(rest, 2)
+    x, core = lax.div(e, 2), lax.rem(e, 2)
+    at_y = (d + 1 - 2 * y, e)
+    at_zlo = (d + 2 - 4 * zlo, e)
+    at_zhi = (d + 4 - 8 * zhi, e)
+    at_core = (d, e + 1 - 2 * core)
+    at_x = (d, e + 2 - 4 * x)
+
+    loads = []
+    for run in range(2):
+        where = pl.ds(pl.multiple_of(run * half + zlo * chunk, 128), chunk)
+        here = pl.ds(run * chunk, chunk)
+        loads.append(pltpu.make_async_copy(w_in.at[0, :, where], wi.at[:, here], w_sem.at[2 * run]))
+        loads.append(pltpu.make_async_copy(w_out.at[0, where, :], wo.at[here, :], w_sem.at[2 * run + 1]))
+    for load in loads:
+        load.start()
+
+    barrier = pltpu.get_barrier_semaphore()
+    for peer in (at_y, at_zlo, at_zhi, at_core, at_x):
+        pl.semaphore_signal(barrier, inc=1, device_id=peer, device_id_type=MESH)
+
+    def slot(s, count=1):
+        return pl.ds(s * tok, count * tok)
+
+    sent = []
+
+    def push(src, dst, send, recv, peer):
+        copy = pltpu.make_async_remote_copy(
+            src_ref=src, dst_ref=dst, send_sem=send, recv_sem=recv,
+            device_id=peer, device_id_type=MESH,
+        )
+        copy.start()
+        sent.append(copy)
+        return copy
+
+    gathered = {}
+
+    def gather_one(kind, src, dst, peer):
+        if kind == 2:
+            a, b = gts.at[src], gts.at[dst]
+        else:
+            buffer = (cots, nrm)[kind]
+            a, b = buffer.at[slot(src)], buffer.at[slot(dst)]
+        gathered[kind, dst] = push(a, b, ag_send.at[kind, dst], ag_recv.at[kind, dst], peer)
+
+    def forward(src, routes):
+        for kind in (0, 1, 2):
+            if src:
+                gathered[kind, src].wait_recv()
+            for dst, peer in routes:
+                gather_one(kind, src, dst, peer)
+
+    first = ((2, at_zlo), (4, at_x), (1, at_core))
+    cots[slot(0)] = cot[...]
+    gts[0] = gates[...]
+    pl.semaphore_wait(barrier, 5)
+    for dst, peer in first:
+        gather_one(0, 0, dst, peer)
+        gather_one(2, 0, dst, peer)
+    nrm[slot(0)] = standardize(frames[...].astype(jnp.float32))[0].astype(jnp.bfloat16)
+    for dst, peer in first:
+        gather_one(1, 0, dst, peer)
+    for load in loads:
+        load.wait()
+
+    eye = lax.broadcasted_iota(jnp.int32, (tok, tok), 0) == lax.broadcasted_iota(jnp.int32, (tok, tok), 1)
+    mine = lax.broadcasted_iota(jnp.int32, gts.shape[1:], 0) == e
+
+    def hidden_pair(p):
+        for s in (2 * p, 2 * p + 1):
+            line = jnp.sum(jnp.where(mine, gts[s], 0.0), axis=0, keepdims=True)
+            column = jnp.sum(jnp.where(eye, jnp.broadcast_to(line, (tok, tok)), 0.0), axis=1, keepdims=True)
+            gcol[slot(s)] = column
+            grow[slot(s)] = (cots[slot(s)].astype(jnp.float32) * column).astype(jnp.bfloat16)
+        block = slot(2 * p, 2)
+
+        def step(j, carry):
+            part = pl.ds(pl.multiple_of(j * tile, tile), tile)
+            pre = dot(nrm[block], wi[:, part], 1, 0)
+            grad = dot(grow[block], wo[part, :], 1, 1)
+            sigma = jax.nn.sigmoid(pre)
+            hid[block, part] = (pre * sigma).astype(jnp.bfloat16)
+            gpre[block, part] = (grad * (sigma + pre * sigma * (1.0 - sigma))).astype(jnp.bfloat16)
+            return carry
+
+        lax.fori_loop(0, half // tile, step, 0)
+
+    forwarded_core = lambda s: ((s + 1, at_core),)
+
+    def wait_slot(s):
+        for kind in (0, 1, 2):
+            gathered[kind, s].wait_recv()
+
+    wait_slot(1)
+    hidden_pair(0)
+    forward(2, ((6, at_x),) + forwarded_core(2))
+    forward(4, forwarded_core(4))
+    wait_slot(3)
+    hidden_pair(1)
+    wait_slot(5)
+    hidden_pair(2)
+    forward(6, forwarded_core(6))
+    wait_slot(7)
+    hidden_pair(3)
+
+    def term_out(zh, yy):
+        part = pl.ds(pl.multiple_of(zh * chunk + yy * h_own, 128), h_own)
+        return dot(hid[:, part], grow[...], 0, 0)
+
+    def term_in(zh, yy, zl):
+        part = pl.ds(pl.multiple_of((4 * zh + 2 * zl + yy) * d_own, 128), d_own)
+        return dot(nrm[:, part], gpre[...], 0, 0)
+
+    def zh_of(dz):
+        return zhi if dz == 0 else 1 - zhi
+
+    def zl_of(dl):
+        return zlo if dl == 0 else 1 - zlo
+
+    d_rows = [pl.ds(dl * d_own, d_own) for dl in range(2)]
+    y_in, y_out = {}, {}
+    for dz in (1, 0):
+        for dl in range(2):
+            syi[dz, d_rows[dl]] = term_in(zh_of(dz), 1 - y, zl_of(dl)).astype(jnp.bfloat16)
+        y_in[dz] = push(syi.at[dz], ryi.at[dz], dw_send.at[dz], dw_recv.at[dz], at_y)
+        syo[dz] = term_out(zh_of(dz), 1 - y).astype(jnp.bfloat16)
+        y_out[dz] = push(syo.at[dz], ryo.at[dz], dw_send.at[2 + dz], dw_recv.at[2 + dz], at_y)
+
+    def back_pair(p):
+        block = slot(2 * p, 2)
+
+        def step(j, carry):
+            part = pl.ds(pl.multiple_of(j * tile, tile), tile)
+            out = dot(hid[block], wo[:, part], 1, 0) * gcol[block]
+            pm[block, part] = out.astype(jnp.bfloat16)
+            pg[block, part] = dot(gpre[block], wi[part, :], 1, 1).astype(jnp.bfloat16)
+            return carry
+
+        lax.fori_loop(0, width // tile, step, 0)
+
+    def give(src, at, peer):
+        return [
+            push(own.at[slot(src)], there.at[slot(at)], rs_send.at[k, at], rs_recv.at[k, at], peer)
+            for k, (own, there) in enumerate(((pm, rm), (pg, rg)))
+        ]
+
+    def take(copies, at, into):
+        for copy, own, there in zip(copies, (pm, pg), (rm, rg)):
+            copy.wait_recv()
+            total = own[slot(into)].astype(jnp.float32) + there[slot(at)].astype(jnp.float32)
+            own[slot(into)] = total.astype(jnp.bfloat16)
+
+    by_core = {}
+    for p in (3, 2, 1, 0):
+        back_pair(p)
+        by_core[p] = give(2 * p + 1, p, at_core)
+    take(by_core[3], 3, 6)
+    by_x = {1: give(6, 5, at_x)}
+    take(by_core[2], 2, 4)
+    by_x[0] = give(4, 4, at_x)
+
+    for dl in range(2):
+        owi[1, d_rows[dl]] = term_in(zh_of(1), y, zl_of(dl))
+    owo[1] = term_out(zh_of(1), y)
+    y_in[1].wait_recv()
+    szi[...] = (owi[1] + ryi[1].astype(jnp.float32)).astype(jnp.bfloat16)
+    z_in = push(szi, rzi, dw_send.at[4], dw_recv.at[4], at_zhi)
+    take(by_core[1], 1, 2)
+    take(by_core[0], 0, 0)
+    y_out[1].wait_recv()
+    szo[...] = (owo[1] + ryo[1].astype(jnp.float32)).astype(jnp.bfloat16)
+    z_out = push(szo, rzo, dw_send.at[5], dw_recv.at[5], at_zhi)
+    for dl in range(2):
+        owi[0, d_rows[dl]] = term_in(zh_of(0), y, zl_of(dl))
+    owo[0] = term_out(zh_of(0), y)
+
+    take(by_x[1], 5, 2)
+    by_zlo = give(2, 6, at_zlo)
+    take(by_x[0], 4, 0)
+
+    y_in[0].wait_recv()
+    owi[0] = owi[0] + ryi[0].astype(jnp.float32)
+    for copy in by_zlo:
+        copy.wait_recv()
+    values = frames[...].astype(jnp.float32)
+    total = pm[slot(0)].astype(jnp.float32) + rm[slot(6)].astype(jnp.float32)
+    mixed[...] = (values + total).astype(jnp.bfloat16)
+    standardized, inverse = standardize(values)
+    grad = pg[slot(0)].astype(jnp.float32) + rg[slot(6)].astype(jnp.float32)
+    centered = grad - jnp.mean(grad, axis=-1, keepdims=True)
+    along = standardized * jnp.mean(grad * standardized, axis=-1, keepdims=True)
+    grad_frames[...] = (cot[...].astype(jnp.float32) + inverse * (centered - along)).astype(jnp.bfloat16)
+
+    z_in.wait_recv()
+    sl[...] = (owi[0, d_rows[1]] + rzi[d_rows[1]].astype(jnp.float32)).astype(jnp.bfloat16)
+    last = push(sl, rl, dw_send.at[6], dw_recv.at[6], at_zlo)
+    y_out[0].wait_recv()
+    final = owi[0, d_rows[0]] + rzi[d_rows[0]].astype(jnp.float32)
+    for run in range(2):
+        where = pl.ds(pl.multiple_of(run * half + zlo * chunk, 128), chunk)
+        grad_w_in[0, :, where] = final[:, run * chunk : (run + 1) * chunk]
+    z_out.wait_recv()
+    grad_w_out[0] = owo[0] + ryo[0].astype(jnp.float32) + rzo[...].astype(jnp.float32)
+    last.wait_recv()
+    for run in range(2):
+        where = pl.ds(pl.multiple_of(run * half + (1 - zlo) * chunk, 128), chunk)
+        grad_w_in[0, :, where] = rl[:, run * chunk : (run + 1) * chunk].astype(jnp.float32)
+    for copy in sent:
+        copy.wait_send()
+
+
+def fused(frames, expert_ids, gate_weights, cotangent, w_in, w_out):
+    tok, width = frames.shape
+    hidden = w_in.shape[2]
+    peers, n_dp = lax.axis_size("expert"), lax.axis_size("dp")
+    half, blocks = hidden // 2, 2 * peers
+    rows, d_own, h_own = blocks * tok, width // n_dp, hidden // n_dp
+    lines = -(-peers // 8) * 8
+    named = expert_ids.T[:, None, :] == jnp.arange(lines, dtype=jnp.int32)[None, :, None]
+    gates = jnp.sum(jnp.where(named, 0.5 * gate_weights.T[:, None, :], 0.0), axis=0)
+    bf, f32 = jnp.bfloat16, jnp.float32
+    vmem = pltpu.VMEM
+    dma = pltpu.SemaphoreType.DMA
+    in_vmem, anywhere = pl.BlockSpec(memory_space=pltpu.VMEM), pl.BlockSpec(memory_space=pl.ANY)
+    return tuple(
+        pl.pallas_call(
+            functools.partial(layer_kernel, min(256, half)),
+            out_shape=(
+                jax.ShapeDtypeStruct((tok, width), bf),
+                jax.ShapeDtypeStruct((tok, width), bf),
+                jax.ShapeDtypeStruct((1, d_own, hidden), f32),
+                jax.ShapeDtypeStruct((1, h_own, width), f32),
+            ),
+            in_specs=[in_vmem] * 3 + [anywhere] * 2,
+            out_specs=(in_vmem,) * 4,
+            scratch_shapes=[
+                vmem((rows, width), bf),
+                vmem((rows, width), bf),
+                vmem((blocks, lines, tok), f32),
+                vmem((rows, 1), f32),
+                vmem((rows, width), bf),
+                vmem((rows, half), bf),
+                vmem((rows, half), bf),
+                vmem((width, half), bf),
+                vmem((half, width), bf),
+                vmem((rows, width), bf),
+                vmem((rows, width), bf),
+                vmem((7 * tok, width), bf),
+                vmem((7 * tok, width), bf),
+                vmem((2, h_own, width), bf),
+                vmem((2, 2 * d_own, half), bf),
+                vmem((2, h_own, width), bf),
+                vmem((2, 2 * d_own, half), bf),
+                vmem((2, h_own, width), f32),
+                vmem((2, 2 * d_own, half), f32),
+                vmem((h_own, width), bf),
+                vmem((2 * d_own, half), bf),
+                vmem((h_own, width), bf),
+                vmem((2 * d_own, half), bf),
+                vmem((d_own, half), bf),
+                vmem((d_own, half), bf),
+                dma((4,)),
+                dma((3, blocks)),
+                dma((3, blocks)),
+                dma((2, 7)),
+                dma((2, 7)),
+                dma((7,)),
+                dma((7,)),
+            ],
+            compiler_params=pltpu.CompilerParams(
+                collective_id=0, has_side_effects=True, vmem_limit_bytes=56 * 2**20
+            ),
+        )(frames, cotangent, gates, w_in, w_out)
+    )
+
+
 def solution(mesh):
+    paired = mesh.shape["expert"] == 2**2 and mesh.shape["dp"] == 2**3
     return jax.shard_map(
-        per_device,
+        fused if paired else per_device,
         mesh=mesh,
         in_specs=(
             P(("dp", "expert"), None),

time: 253 us -> 113 us (0.45)
  waiting for transfers between devices: 149 us -> 0 us
  Pallas kernels: 0 us -> 102 us
  matrix products: 36.5 us -> 0 us
  starting transfers between devices: 15.2 us -> 0 us
  local copies, waits for them, and re-layouts: 22.6 us -> 7.94 us
  between operations: 14.3 us -> 0.64 us
  other arithmetic: 14.7 us -> 1.96 us
    pallas_call x0 -> x1, Pallas kernels: none -> 102 us  [fused(): pl.pallas_call(functools.partial(layer_kernel, min(256, half)), out_shape...]
    unnamed x3 -> x0, waiting for transfers between devices: 89.5 us -> none
    all_to_all x4 -> x0, waiting for transfers between devices: 40.2 us -> none  [route_rows(): lax.all_to_all(buffer, 'expert', split_axis=0, concat_axis=0, tiled=True)]
    dot_general x6 -> x0, matrix products: 36.5 us -> none  [the longest x1 7.03 us: per_device(): jnp.einsum('sech,ehd->secd', hidden, w_out, preferred_element_type=jnp.fl...]
    reduce_scatter x1 -> x0, waiting for transfers between devices: 18.8 us -> none  [per_device(): lax.psum_scatter(jnp.einsum('sech,secd->hed', piece, grad_recv, preferred...]
    all_to_all x4 -> x0, starting transfers between devices: 15 us -> none  [route_rows(): lax.all_to_all(buffer, 'expert', split_axis=0, concat_axis=0, tiled=True)]
    unnamed x16 -> x4, local copies, waits for them, and re-layouts: 12.6 us -> 7.94 us
    reduce_sum x8 -> x1, other arithmetic: 5.39 us -> 1.28 us  [fused(): jnp.sum(jnp.where(named, 0.5 * gate_weights.T[:, None, :], 0.0), axis=0)]
  transfers between devices with their start and end apart: 6 -> 0, of which waited for: 6 -> 0; matrix products, arithmetic and copies ran while one was open for 21% -> 0% of each run, Pallas kernels for 0% -> 0%
where the time goes in v1:
time: 113 us
  Pallas kernels  102 us (90%)
  local copies, waits for them, and re-layouts  7.94 us (7%)
  other arithmetic  1.96 us (2%)
    pallas_call x1, Pallas kernels, fused(): pl.pallas_call(functools.partial(layer_kernel, min(256, half)), out_shape...  102 us
    unnamed x4, local copies, waits for them, and re-layouts  7.94 us

profile of v1, /device:TPU:0, one launch (start us, length us, event | category | flops | bytes accessed | tf_op | source)
XLA Modules:
  0.0 112.8 jit_solution(8672280191224081159)
XLA Ops:
  0.6 0.7 multiply_bitcast_fusion
  1.3 1.3 %select_reduce_fusion.gates = f32[8,128]{1,0:T(8,128)} fusion(f32[2,128]{1,0:T(2,128)S(1)} %multiply_bitcast_fusion, s32[2,128]{1,0:T(2,128)} %bitcast.3), kind=kLoop, calls=%fused_computation | loop fusion | flops 5120 | bytes 6144 | tf_op jit(solution)/shard_map/reduce_sum | solution.py:362
  2.6 102.3 %shard_map.93 = (bf16[128,1024]{1,0:T(8,128)(2,1)}, bf16[128,1024]{1,0:T(8,128)(2,1)}, f32[1,128,2048]{2,1,0:T(8,128)}, f32[1,256,1024]{2,1,0:T(8,128)}) custom-call(bf16[128,1024]{1,0:T(8,128)(2,1)} %frames.1, bf16[128,1024]{1,0:T(8,128)(2,1)} %cot.1, f32[8,128]{1,0:T(8,128)} %select_reduce_fusion.gates, bf16[1,1024,2048]{2,1,0:T(8,128)(2,1)} %w_in.1, ...), custom_call_target="tpu_custom_call" | custom-call | tf_op jit(solution)/shard_map/pallas_call | solution.py:368
  104.9 1.7 %copy.14 = bf16[128,1024]{1,0:T(8,128)(2,1)} copy(bf16[128,1024]{1,0:T(8,128)(2,1)} %get-tuple-element.8) | data formatting | bytes 524288
  106.5 1.7 %copy.15 = bf16[128,1024]{1,0:T(8,128)(2,1)} copy(bf16[128,1024]{1,0:T(8,128)(2,1)} %get-tuple-element.9) | data formatting | bytes 524288
  108.2 2.3 %copy.16 = f32[1,128,2048]{2,1,0:T(8,128)} copy(f32[1,128,2048]{2,1,0:T(8,128)} %get-tuple-element.10) | data formatting | bytes 2097152
  110.5 2.3 %copy.17 = f32[1,256,1024]{2,1,0:T(8,128)} copy(f32[1,256,1024]{2,1,0:T(8,128)} %get-tuple-element.11) | data formatting | bytes 2097152

commit v2 on v1

--- a/solution.py
+++ b/solution.py
@@ -125,11 +125,11 @@
 
 def layer_kernel(
     tile,
-    frames, cot, gates, w_in, w_out,
+    frames, cot, ids, gates, w_in, w_out,
     mixed, grad_frames, grad_w_in, grad_w_out,
     nrm, cots, gts, gcol, grow, hid, gpre, wi, wo, pm, pg, rm, rg,
     syo, syi, ryo, ryi, owo, owi, szo, szi, rzo, rzi, sl, rl,
-    w_sem, ag_send, ag_recv, rs_send, rs_recv, dw_send, dw_recv,
+    w_sem, ag_send, ag_recv, rs_send, rs_recv, y_send, y_recv, z_send, z_recv, l_send, l_recv,
 ):
     tok, width = frames.shape
     rows = nrm.shape[0]
@@ -185,28 +185,32 @@
             a, b = buffer.at[slot(src)], buffer.at[slot(dst)]
         gathered[kind, dst] = push(a, b, ag_send.at[kind, dst], ag_recv.at[kind, dst], peer)
 
-    def forward(src, routes):
-        for kind in (0, 1, 2):
+    def forward(kinds, src, routes):
+        for kind in kinds:
             if src:
                 gathered[kind, src].wait_recv()
             for dst, peer in routes:
                 gather_one(kind, src, dst, peer)
 
-    first = ((2, at_zlo), (4, at_x), (1, at_core))
+    line_of = lax.broadcasted_iota(jnp.int32, gts.shape[1:], 0)
     cots[slot(0)] = cot[...]
-    gts[0] = gates[...]
+    gts[0] = sum(
+        jnp.where(line_of == ids[k : k + 1, :], 0.5 * gates[k : k + 1, :], 0.0)
+        for k in range(ids.shape[0])
+    )
+    nrm[slot(0)] = standardize(frames[...].astype(jnp.float32))[0].astype(jnp.bfloat16)
     pl.semaphore_wait(barrier, 5)
-    for dst, peer in first:
-        gather_one(0, 0, dst, peer)
-        gather_one(2, 0, dst, peer)
-    nrm[slot(0)] = standardize(frames[...].astype(jnp.float32))[0].astype(jnp.bfloat16)
-    for dst, peer in first:
-        gather_one(1, 0, dst, peer)
+    forward((0,), 0, ((2, at_zlo),))
+    forward((1,), 0, ((4, at_x),))
+    forward((2,), 0, ((2, at_zlo), (4, at_x), (1, at_core)))
+    forward((0, 1), 0, ((1, at_core),))
+    forward((1,), 0, ((2, at_zlo),))
+    forward((0,), 0, ((4, at_x),))
     for load in loads:
         load.wait()
 
     eye = lax.broadcasted_iota(jnp.int32, (tok, tok), 0) == lax.broadcasted_iota(jnp.int32, (tok, tok), 1)
-    mine = lax.broadcasted_iota(jnp.int32, gts.shape[1:], 0) == e
+    mine = line_of == e
 
     def hidden_pair(p):
         for s in (2 * p, 2 * p + 1):
@@ -227,46 +231,23 @@
 
         lax.fori_loop(0, half // tile, step, 0)
 
-    forwarded_core = lambda s: ((s + 1, at_core),)
-
     def wait_slot(s):
         for kind in (0, 1, 2):
             gathered[kind, s].wait_recv()
 
     wait_slot(1)
     hidden_pair(0)
-    forward(2, ((6, at_x),) + forwarded_core(2))
-    forward(4, forwarded_core(4))
+    forward((2, 0), 2, ((6, at_x), (3, at_core)))
+    forward((1,), 4, ((6, at_zlo), (5, at_core)))
+    forward((1,), 2, ((3, at_core),))
+    forward((2, 0), 4, ((5, at_core),))
     wait_slot(3)
     hidden_pair(1)
     wait_slot(5)
     hidden_pair(2)
-    forward(6, forwarded_core(6))
+    forward((2, 0, 1), 6, ((7, at_core),))
     wait_slot(7)
     hidden_pair(3)
-
-    def term_out(zh, yy):
-        part = pl.ds(pl.multiple_of(zh * chunk + yy * h_own, 128), h_own)
-        return dot(hid[:, part], grow[...], 0, 0)
-
-    def term_in(zh, yy, zl):
-        part = pl.ds(pl.multiple_of((4 * zh + 2 * zl + yy) * d_own, 128), d_own)
-        return dot(nrm[:, part], gpre[...], 0, 0)
-
-    def zh_of(dz):
-        return zhi if dz == 0 else 1 - zhi
-
-    def zl_of(dl):
-        return zlo if dl == 0 else 1 - zlo
-
-    d_rows = [pl.ds(dl * d_own, d_own) for dl in range(2)]
-    y_in, y_out = {}, {}
-    for dz in (1, 0):
-        for dl in range(2):
-            syi[dz, d_rows[dl]] = term_in(zh_of(dz), 1 - y, zl_of(dl)).astype(jnp.bfloat16)
-        y_in[dz] = push(syi.at[dz], ryi.at[dz], dw_send.at[dz], dw_recv.at[dz], at_y)
-        syo[dz] = term_out(zh_of(dz), 1 - y).astype(jnp.bfloat16)
-        y_out[dz] = push(syo.at[dz], ryo.at[dz], dw_send.at[2 + dz], dw_recv.at[2 + dz], at_y)
 
     def back_pair(p):
         block = slot(2 * p, 2)
@@ -280,50 +261,111 @@
 
         lax.fori_loop(0, width // tile, step, 0)
 
-    def give(src, at, peer):
-        return [
-            push(own.at[slot(src)], there.at[slot(at)], rs_send.at[k, at], rs_recv.at[k, at], peer)
-            for k, (own, there) in enumerate(((pm, rm), (pg, rg)))
-        ]
-
-    def take(copies, at, into):
-        for copy, own, there in zip(copies, (pm, pg), (rm, rg)):
-            copy.wait_recv()
-            total = own[slot(into)].astype(jnp.float32) + there[slot(at)].astype(jnp.float32)
-            own[slot(into)] = total.astype(jnp.bfloat16)
+    def give(k, src, at, peer):
+        own, there = ((pm, rm), (pg, rg))[k]
+        return push(own.at[slot(src)], there.at[slot(at)], rs_send.at[k, at], rs_recv.at[k, at], peer)
+
+    def take(k, copy, at, into):
+        own, there = ((pm, rm), (pg, rg))[k]
+        copy.wait_recv()
+        total = own[slot(into)].astype(jnp.float32) + there[slot(at)].astype(jnp.float32)
+        own[slot(into)] = total.astype(jnp.bfloat16)
+
+    h_part = h_own // 2
+
+    def piece(n, zh, yy):
+        if n < 2:
+            zl = zlo if n else 1 - zlo
+            part = pl.ds(pl.multiple_of((4 * zh + 2 * zl + yy) * d_own, 128), d_own)
+            return dot(nrm[:, part], gpre[...], 0, 0)
+        part = pl.ds(pl.multiple_of(zh * chunk + yy * h_own + (n - 2) * h_part, 128), h_part)
+        return dot(hid[:, part], grow[...], 0, 0)
+
+    def split(n, buffers):
+        rows_of = d_own if n < 2 else h_part
+        return buffers[n // 2], pl.ds(n % 2 * rows_of, rows_of)
+
+    to_y, to_z = {}, {}
+
+    def send_y(n, dz):
+        src, at = split(n, (syi, syo))
+        dst, _ = split(n, (ryi, ryo))
+        src[dz, at] = piece(n, zhi if dz == 0 else 1 - zhi, 1 - y).astype(jnp.bfloat16)
+        to_y[n, dz] = push(
+            src.at[dz, at], dst.at[dz, at], y_send.at[dz, n], y_recv.at[dz, n], at_y
+        )
+
+    def keep(n, dz):
+        own, at = split(n, (owi, owo))
+        own[dz, at] = piece(n, zhi if dz == 0 else 1 - zhi, y)
+
+    def over_y(n, dz):
+        own, at = split(n, (owi, owo))
+        got, _ = split(n, (ryi, ryo))
+        to_y[n, dz].wait_recv()
+        return own[dz, at] + got[dz, at].astype(jnp.float32)
+
+    def send_z(n):
+        src, at = split(n, (szi, szo))
+        dst, _ = split(n, (rzi, rzo))
+        src[at] = over_y(n, 1).astype(jnp.bfloat16)
+        to_z[n] = push(src.at[at], dst.at[at], z_send.at[n], z_recv.at[n], at_zhi)
+
+    def finish(n):
+        got, at = split(n, (rzi, rzo))
+        total = over_y(n, 0)
+        to_z[n].wait_recv()
+        return total + got[at].astype(jnp.float32)
 
     by_core = {}
-    for p in (3, 2, 1, 0):
+
+    def back_and_give(p):
         back_pair(p)
-        by_core[p] = give(2 * p + 1, p, at_core)
-    take(by_core[3], 3, 6)
-    by_x = {1: give(6, 5, at_x)}
-    take(by_core[2], 2, 4)
-    by_x[0] = give(4, 4, at_x)
-
-    for dl in range(2):
-        owi[1, d_rows[dl]] = term_in(zh_of(1), y, zl_of(dl))
-    owo[1] = term_out(zh_of(1), y)
-    y_in[1].wait_recv()
-    szi[...] = (owi[1] + ryi[1].astype(jnp.float32)).astype(jnp.bfloat16)
-    z_in = push(szi, rzi, dw_send.at[4], dw_recv.at[4], at_zhi)
-    take(by_core[1], 1, 2)
-    take(by_core[0], 0, 0)
-    y_out[1].wait_recv()
-    szo[...] = (owo[1] + ryo[1].astype(jnp.float32)).astype(jnp.bfloat16)
-    z_out = push(szo, rzo, dw_send.at[5], dw_recv.at[5], at_zhi)
-    for dl in range(2):
-        owi[0, d_rows[dl]] = term_in(zh_of(0), y, zl_of(dl))
-    owo[0] = term_out(zh_of(0), y)
-
-    take(by_x[1], 5, 2)
-    by_zlo = give(2, 6, at_zlo)
-    take(by_x[0], 4, 0)
-
-    y_in[0].wait_recv()
-    owi[0] = owi[0] + ryi[0].astype(jnp.float32)
-    for copy in by_zlo:
-        copy.wait_recv()
+        for k in range(2):
+            by_core[k, p] = give(k, 2 * p + 1, p, at_core)
+
+    for n in range(4):
+        send_y(n, 1)
+    for n in range(4):
+        keep(n, 1)
+    back_and_give(3)
+    send_z(0)
+    back_and_give(2)
+    take(0, by_core[0, 3], 3, 6)
+    x_m2 = give(0, 6, 5, at_x)
+    take(1, by_core[1, 3], 3, 6)
+    z_g4 = give(1, 6, 5, at_zlo)
+    send_z(1)
+    send_y(0, 0)
+    send_y(1, 0)
+    back_and_give(1)
+    take(0, by_core[0, 2], 2, 4)
+    x_m0 = give(0, 4, 4, at_x)
+    send_z(2)
+    send_y(2, 0)
+    send_y(3, 0)
+    back_and_give(0)
+    take(1, by_core[1, 1], 1, 2)
+    z_g0 = give(1, 2, 4, at_zlo)
+    send_z(3)
+    take(1, by_core[1, 2], 2, 4)
+    take(0, by_core[0, 1], 1, 2)
+    take(0, by_core[0, 0], 0, 0)
+    take(1, by_core[1, 0], 0, 0)
+    take(0, x_m2, 5, 2)
+    z_m0 = give(0, 2, 6, at_zlo)
+    take(1, z_g4, 5, 4)
+    x_g0 = give(1, 4, 6, at_x)
+    for n in range(4):
+        keep(n, 0)
+    take(0, x_m0, 4, 0)
+    take(1, z_g0, 4, 0)
+
+    sl[...] = finish(0).astype(jnp.bfloat16)
+    last = push(sl, rl, l_send, l_recv, at_zlo)
+
+    z_m0.wait_recv()
+    x_g0.wait_recv()
     values = frames[...].astype(jnp.float32)
     total = pm[slot(0)].astype(jnp.float32) + rm[slot(6)].astype(jnp.float32)
     mixed[...] = (values + total).astype(jnp.bfloat16)
@@ -333,22 +375,28 @@
     along = standardized * jnp.mean(grad * standardized, axis=-1, keepdims=True)
     grad_frames[...] = (cot[...].astype(jnp.float32) + inverse * (centered - along)).astype(jnp.bfloat16)
 
-    z_in.wait_recv()
-    sl[...] = (owi[0, d_rows[1]] + rzi[d_rows[1]].astype(jnp.float32)).astype(jnp.bfloat16)
-    last = push(sl, rl, dw_send.at[6], dw_recv.at[6], at_zlo)
-    y_out[0].wait_recv()
-    final = owi[0, d_rows[0]] + rzi[d_rows[0]].astype(jnp.float32)
+    final = finish(1)
     for run in range(2):
         where = pl.ds(pl.multiple_of(run * half + zlo * chunk, 128), chunk)
         grad_w_in[0, :, where] = final[:, run * chunk : (run + 1) * chunk]
-    z_out.wait_recv()
-    grad_w_out[0] = owo[0] + ryo[0].astype(jnp.float32) + rzo[...].astype(jnp.float32)
+    grad_w_out[0, :h_part] = finish(2)
     last.wait_recv()
     for run in range(2):
         where = pl.ds(pl.multiple_of(run * half + (1 - zlo) * chunk, 128), chunk)
         grad_w_in[0, :, where] = rl[:, run * chunk : (run + 1) * chunk].astype(jnp.float32)
+    grad_w_out[0, h_part:] = finish(3)
     for copy in sent:
         copy.wait_send()
+
+
+def hand_on(*refs):
+    count = len(refs) // 2
+    sources, targets, sems = refs[:count], refs[count:-1], refs[-1]
+    copies = [pltpu.make_async_copy(a, b, sems.at[i]) for i, (a, b) in enumerate(zip(sources, targets))]
+    for copy in copies:
+        copy.start()
+    for copy in copies:
+        copy.wait()
 
 
 def fused(frames, expert_ids, gate_weights, cotangent, w_in, w_out):
@@ -358,13 +406,11 @@
     half, blocks = hidden // 2, 2 * peers
     rows, d_own, h_own = blocks * tok, width // n_dp, hidden // n_dp
     lines = -(-peers // 8) * 8
-    named = expert_ids.T[:, None, :] == jnp.arange(lines, dtype=jnp.int32)[None, :, None]
-    gates = jnp.sum(jnp.where(named, 0.5 * gate_weights.T[:, None, :], 0.0), axis=0)
     bf, f32 = jnp.bfloat16, jnp.float32
     vmem = pltpu.VMEM
     dma = pltpu.SemaphoreType.DMA
     in_vmem, anywhere = pl.BlockSpec(memory_space=pltpu.VMEM), pl.BlockSpec(memory_space=pl.ANY)
-    return tuple(
+    results = tuple(
         pl.pallas_call(
             functools.partial(layer_kernel, min(256, half)),
             out_shape=(
@@ -373,7 +419,7 @@
                 jax.ShapeDtypeStruct((1, d_own, hidden), f32),
                 jax.ShapeDtypeStruct((1, h_own, width), f32),
             ),
-            in_specs=[in_vmem] * 3 + [anywhere] * 2,
+            in_specs=[in_vmem] * 4 + [anywhere] * 2,
             out_specs=(in_vmem,) * 4,
             scratch_shapes=[
                 vmem((rows, width), bf),
@@ -406,13 +452,26 @@
                 dma((3, blocks)),
                 dma((2, 7)),
                 dma((2, 7)),
-                dma((7,)),
-                dma((7,)),
+                dma((2, 4)),
+                dma((2, 4)),
+                dma((4,)),
+                dma((4,)),
+                dma(()),
+                dma(()),
             ],
             compiler_params=pltpu.CompilerParams(
                 collective_id=0, has_side_effects=True, vmem_limit_bytes=56 * 2**20
             ),
-        )(frames, cotangent, gates, w_in, w_out)
+        )(frames, cotangent, expert_ids.T, gate_weights.T, w_in, w_out)
+    )
+    return tuple(
+        pl.pallas_call(
+            hand_on,
+            out_shape=tuple(jax.ShapeDtypeStruct(r.shape, r.dtype) for r in results),
+            in_specs=[anywhere] * 4,
+            out_specs=(anywhere,) * 4,
+            scratch_shapes=[dma((4,))],
+        )(*results)
     )
 
 

time: 113 us -> 170 us (1.50)
  Pallas kernels: 102 us -> 169 us
  local copies, waits for them, and re-layouts: 7.94 us -> 0 us
  other arithmetic: 1.96 us -> 0 us
    pallas_call x0 -> x1, Pallas kernels: none -> 80.5 us  [fused(): pl.pallas_call(hand_on, out_shape=tuple((jax.ShapeDtypeStruct(r.shape, r....]
    pallas_call x1, Pallas kernels: 102 us -> 88.5 us  [fused(): pl.pallas_call(functools.partial(layer_kernel, min(256, half)), out_shape...]
    unnamed x4 -> x0, local copies, waits for them, and re-layouts: 7.94 us -> none
where the time goes in v2:
time: 170 us
  Pallas kernels  169 us (99%)
    pallas_call x1, Pallas kernels, fused(): pl.pallas_call(functools.partial(layer_kernel, min(256, half)), out_shape...  88.5 us
    pallas_call x1, Pallas kernels, fused(): pl.pallas_call(hand_on, out_shape=tuple((jax.ShapeDtypeStruct(r.shape, r....  80.5 us

profile of v2, /device:TPU:0, one launch (start us, length us, event | category | flops | bytes accessed | tf_op | source)
XLA Modules:
  0.0 169.7 jit_solution(11472428874638845262)
XLA Ops:
  0.6 88.5 %shard_map.93 = (bf16[128,1024]{1,0:T(8,128)(2,1)}, bf16[128,1024]{1,0:T(8,128)(2,1)}, f32[1,128,2048]{2,1,0:T(8,128)}, f32[1,256,1024]{2,1,0:T(8,128)}) custom-call(bf16[128,1024]{1,0:T(8,128)(2,1)} %frames.1, bf16[128,1024]{1,0:T(8,128)(2,1)} %cot.1, s32[2,128]{1,0:T(2,128)} %bitcast.2, f32[2,128]{1,0:T(2,128)} %bitcast.3, bf16[1,1024,2048]{2,1,0:T(8,128)(2,1)} %w_in.1, ...), custom_call_target="tpu_custom_call" | custom-call | tf_op jit(solution)/shard_map/pallas_call | solution.py:414
  89.1 80.5 %shard_map.94 = (bf16[128,1024]{1,0:T(8,128)(2,1)}, bf16[128,1024]{1,0:T(8,128)(2,1)}, f32[1,128,2048]{2,1,0:T(8,128)}, f32[1,256,1024]{2,1,0:T(8,128)}) custom-call(bf16[128,1024]{1,0:T(8,128)(2,1)} %get-tuple-element.8.refs_0_, bf16[128,1024]{1,0:T(8,128)(2,1)} %get-tuple-element.9.refs_1_, f32[1,128,2048]{2,1,0:T(8,128)} %get-tuple-element.10.refs_2_, ...), custom_call_target="tpu_custom_call" | custom-call | tf_op jit(solution)/shard_map/pallas_call | solution.py:468

commit v3 on v2

--- a/solution.py
+++ b/solution.py
@@ -137,7 +137,7 @@
     chunk = half // 2
     h_own = grad_w_out.shape[1]
     d_own = grad_w_in.shape[1]
-    pairs = rows // (2 * tok)
+    blocks = rows // tok
     d, e = lax.axis_index("dp"), lax.axis_index("expert")
     zhi, rest = lax.div(d, 4), lax.rem(d, 4)
     zlo, y = lax.div(rest, 2), lax.rem(rest, 2)
@@ -235,8 +235,95 @@
         for kind in (0, 1, 2):
             gathered[kind, s].wait_recv()
 
+    def back_pair(p):
+        block = slot(2 * p, 2)
+
+        def step(j, carry):
+            part = pl.ds(pl.multiple_of(j * tile, tile), tile)
+            out = dot(hid[block], wo[:, part], 1, 0) * gcol[block]
+            pm[block, part] = out.astype(jnp.bfloat16)
+            pg[block, part] = dot(gpre[block], wi[part, :], 1, 1).astype(jnp.bfloat16)
+            return carry
+
+        lax.fori_loop(0, width // tile, step, 0)
+
+    def give(k, src, at, peer):
+        own, there = ((pm, rm), (pg, rg))[k]
+        return push(own.at[slot(src)], there.at[slot(at)], rs_send.at[k, at], rs_recv.at[k, at], peer)
+
+    def take(k, copy, at, into):
+        own, there = ((pm, rm), (pg, rg))[k]
+        copy.wait_recv()
+        total = own[slot(into)].astype(jnp.float32) + there[slot(at)].astype(jnp.float32)
+        own[slot(into)] = total.astype(jnp.bfloat16)
+
+    by_core = {}
+
+    def back_and_give(p):
+        back_pair(p)
+        for k in range(2):
+            by_core[k, p] = give(k, 2 * p + 1, p, at_core)
+
+    h_part = h_own // 2
+    early, late = slot(0, blocks - 2), slot(blocks - 2, 2)
+
+    def term(kind, dz, dy, some):
+        zh = zhi if dz == 0 else 1 - zhi
+        yy = y if dy == 0 else 1 - y
+        if kind == 0:
+            parts = [
+                nrm[some, pl.ds(pl.multiple_of((4 * zh + 2 * zl + yy) * d_own, 128), d_own)]
+                for zl in (1 - zlo, zlo)
+            ]
+            return dot(jnp.concatenate(parts, axis=1), gpre[some], 0, 0)
+        part = pl.ds(pl.multiple_of(zh * chunk + yy * h_own, 128), h_own)
+        return dot(hid[some, part], grow[some], 0, 0)
+
+    sums = (owi, owo)
+
+    def begin(kind, dz, dy):
+        sums[kind][dy, dz] = term(kind, dz, dy, early)
+
+    def keep(kind, dz):
+        sums[kind][0, dz] = sums[kind][0, dz] + term(kind, dz, 0, late)
+
+    def split(n, buffers):
+        rows_of = d_own if n < 2 else h_part
+        return buffers[n // 2], pl.ds(n % 2 * rows_of, rows_of)
+
+    to_y, to_z = {}, {}
+
+    def send_y(kind, dz):
+        total = sums[kind][1, dz] + term(kind, dz, 1, late)
+        (syi, syo)[kind][dz] = total.astype(jnp.bfloat16)
+        for n in (2 * kind, 2 * kind + 1):
+            src, at = split(n, (syi, syo))
+            dst, _ = split(n, (ryi, ryo))
+            to_y[n, dz] = push(
+                src.at[dz, at], dst.at[dz, at], y_send.at[dz, n], y_recv.at[dz, n], at_y
+            )
+
+    def over_y(n, dz):
+        own, at = split(n, sums)
+        got, _ = split(n, (ryi, ryo))
+        to_y[n, dz].wait_recv()
+        return own[0, dz, at] + got[dz, at].astype(jnp.float32)
+
+    def send_z(n):
+        src, at = split(n, (szi, szo))
+        dst, _ = split(n, (rzi, rzo))
+        src[at] = over_y(n, 1).astype(jnp.bfloat16)
+        to_z[n] = push(src.at[at], dst.at[at], z_send.at[n], z_recv.at[n], at_zhi)
+
+    def finish(n):
+        got, at = split(n, (rzi, rzo))
+        total = over_y(n, 0)
+        to_z[n].wait_recv()
+        return total + got[at].astype(jnp.float32)
+
     wait_slot(1)
     hidden_pair(0)
+    back_and_give(0)
     forward((2, 0), 2, ((6, at_x), (3, at_core)))
     forward((1,), 4, ((6, at_zlo), (5, at_core)))
     forward((1,), 2, ((3, at_core),))
@@ -245,89 +332,19 @@
     hidden_pair(1)
     wait_slot(5)
     hidden_pair(2)
+    for kind in range(2):
+        begin(kind, 1, 1)
     forward((2, 0, 1), 6, ((7, at_core),))
+    for dz, dy in ((1, 0), (0, 1), (0, 0)):
+        for kind in range(2):
+            begin(kind, dz, dy)
     wait_slot(7)
     hidden_pair(3)
 
-    def back_pair(p):
-        block = slot(2 * p, 2)
-
-        def step(j, carry):
-            part = pl.ds(pl.multiple_of(j * tile, tile), tile)
-            out = dot(hid[block], wo[:, part], 1, 0) * gcol[block]
-            pm[block, part] = out.astype(jnp.bfloat16)
-            pg[block, part] = dot(gpre[block], wi[part, :], 1, 1).astype(jnp.bfloat16)
-            return carry
-
-        lax.fori_loop(0, width // tile, step, 0)
-
-    def give(k, src, at, peer):
-        own, there = ((pm, rm), (pg, rg))[k]
-        return push(own.at[slot(src)], there.at[slot(at)], rs_send.at[k, at], rs_recv.at[k, at], peer)
-
-    def take(k, copy, at, into):
-        own, there = ((pm, rm), (pg, rg))[k]
-        copy.wait_recv()
-        total = own[slot(into)].astype(jnp.float32) + there[slot(at)].astype(jnp.float32)
-        own[slot(into)] = total.astype(jnp.bfloat16)
-
-    h_part = h_own // 2
-
-    def piece(n, zh, yy):
-        if n < 2:
-            zl = zlo if n else 1 - zlo
-            part = pl.ds(pl.multiple_of((4 * zh + 2 * zl + yy) * d_own, 128), d_own)
-            return dot(nrm[:, part], gpre[...], 0, 0)
-        part = pl.ds(pl.multiple_of(zh * chunk + yy * h_own + (n - 2) * h_part, 128), h_part)
-        return dot(hid[:, part], grow[...], 0, 0)
-
-    def split(n, buffers):
-        rows_of = d_own if n < 2 else h_part
-        return buffers[n // 2], pl.ds(n % 2 * rows_of, rows_of)
-
-    to_y, to_z = {}, {}
-
-    def send_y(n, dz):
-        src, at = split(n, (syi, syo))
-        dst, _ = split(n, (ryi, ryo))
-        src[dz, at] = piece(n, zhi if dz == 0 else 1 - zhi, 1 - y).astype(jnp.bfloat16)
-        to_y[n, dz] = push(
-            src.at[dz, at], dst.at[dz, at], y_send.at[dz, n], y_recv.at[dz, n], at_y
-        )
-
-    def keep(n, dz):
-        own, at = split(n, (owi, owo))
-        own[dz, at] = piece(n, zhi if dz == 0 else 1 - zhi, y)
-
-    def over_y(n, dz):
-        own, at = split(n, (owi, owo))
-        got, _ = split(n, (ryi, ryo))
-        to_y[n, dz].wait_recv()
-        return own[dz, at] + got[dz, at].astype(jnp.float32)
-
-    def send_z(n):
-        src, at = split(n, (szi, szo))
-        dst, _ = split(n, (rzi, rzo))
-        src[at] = over_y(n, 1).astype(jnp.bfloat16)
-        to_z[n] = push(src.at[at], dst.at[at], z_send.at[n], z_recv.at[n], at_zhi)
-
-    def finish(n):
-        got, at = split(n, (rzi, rzo))
-        total = over_y(n, 0)
-        to_z[n].wait_recv()
-        return total + got[at].astype(jnp.float32)
-
-    by_core = {}
-
-    def back_and_give(p):
-        back_pair(p)
-        for k in range(2):
-            by_core[k, p] = give(k, 2 * p + 1, p, at_core)
-
-    for n in range(4):
-        send_y(n, 1)
-    for n in range(4):
-        keep(n, 1)
+    for kind in range(2):
+        send_y(kind, 1)
+    for kind in range(2):
+        keep(kind, 1)
     back_and_give(3)
     send_z(0)
     back_and_give(2)
@@ -337,14 +354,11 @@
     z_g4 = give(1, 6, 5, at_zlo)
     send_z(1)
     send_y(0, 0)
-    send_y(1, 0)
     back_and_give(1)
     take(0, by_core[0, 2], 2, 4)
     x_m0 = give(0, 4, 4, at_x)
     send_z(2)
-    send_y(2, 0)
-    send_y(3, 0)
-    back_and_give(0)
+    send_y(1, 0)
     take(1, by_core[1, 1], 1, 2)
     z_g0 = give(1, 2, 4, at_zlo)
     send_z(3)
@@ -356,8 +370,8 @@
     z_m0 = give(0, 2, 6, at_zlo)
     take(1, z_g4, 5, 4)
     x_g0 = give(1, 4, 6, at_x)
-    for n in range(4):
-        keep(n, 0)
+    for kind in range(2):
+        keep(kind, 0)
     take(0, x_m0, 4, 0)
     take(1, z_g0, 4, 0)
 
@@ -391,12 +405,8 @@
 
 def hand_on(*refs):
     count = len(refs) // 2
-    sources, targets, sems = refs[:count], refs[count:-1], refs[-1]
-    copies = [pltpu.make_async_copy(a, b, sems.at[i]) for i, (a, b) in enumerate(zip(sources, targets))]
-    for copy in copies:
-        copy.start()
-    for copy in copies:
-        copy.wait()
+    for source, target in zip(refs[:count], refs[count:]):
+        target[...] = source[...]
 
 
 def fused(frames, expert_ids, gate_weights, cotangent, w_in, w_out):
@@ -439,8 +449,8 @@
                 vmem((2, 2 * d_own, half), bf),
                 vmem((2, h_own, width), bf),
                 vmem((2, 2 * d_own, half), bf),
-                vmem((2, h_own, width), f32),
-                vmem((2, 2 * d_own, half), f32),
+                vmem((2, 2, h_own, width), f32),
+                vmem((2, 2, 2 * d_own, half), f32),
                 vmem((h_own, width), bf),
                 vmem((2 * d_own, half), bf),
                 vmem((h_own, width), bf),
@@ -460,7 +470,7 @@
                 dma(()),
             ],
             compiler_params=pltpu.CompilerParams(
-                collective_id=0, has_side_effects=True, vmem_limit_bytes=56 * 2**20
+                collective_id=0, has_side_effects=True, vmem_limit_bytes=48 * 2**20
             ),
         )(frames, cotangent, expert_ids.T, gate_weights.T, w_in, w_out)
     )
@@ -468,9 +478,8 @@
         pl.pallas_call(
             hand_on,
             out_shape=tuple(jax.ShapeDtypeStruct(r.shape, r.dtype) for r in results),
-            in_specs=[anywhere] * 4,
-            out_specs=(anywhere,) * 4,
-            scratch_shapes=[dma((4,))],
+            in_specs=[in_vmem] * 4,
+            out_specs=(in_vmem,) * 4,
         )(*results)
     )
 

time: 170 us -> 98.3 us (0.58)
  Pallas kernels: 169 us -> 90.7 us
  local copies, waits for them, and re-layouts: 0 us -> 6.64 us
    pallas_call x1, Pallas kernels: 80.5 us -> 3.21 us  [fused(): pl.pallas_call(hand_on, out_shape=tuple((jax.ShapeDtypeStruct(r.shape, r....]
    unnamed x0 -> x16, local copies, waits for them, and re-layouts: none -> 6.64 us
where the time goes in v3:
time: 98.3 us; the launch traced here: 98 us
  Pallas kernels  90.7 us (92%)
  local copies, waits for them, and re-layouts  6.64 us (7%)
    pallas_call x1, Pallas kernels, fused(): pl.pallas_call(functools.partial(layer_kernel, min(256, half)), out_shape...  87.5 us
    unnamed x16, local copies, waits for them, and re-layouts  6.64 us
    pallas_call x1, Pallas kernels, fused(): pl.pallas_call(hand_on, out_shape=tuple((jax.ShapeDtypeStruct(r.shape, r....  3.21 us

profile of v3, /device:TPU:0, one launch (start us, length us, event | category | flops | bytes accessed | tf_op | source)
XLA Modules:
  0.0 98.0 jit_solution(7405637106013457213)
XLA Ops:
  0.6 0.0 copy-start.2
  0.6 0.9 copy-done.2
  1.6 0.0 copy-start.3
  1.6 0.9 copy-done.3
  2.5 0.0 copy-start.6
  2.5 0.7 copy-done.6
  3.2 0.0 copy-start.7
  3.2 0.7 copy-done.7
  3.9 87.5 %shard_map.93 = (bf16[128,1024]{1,0:T(8,128)(2,1)S(1)}, bf16[128,1024]{1,0:T(8,128)(2,1)S(1)}, f32[1,128,2048]{2,1,0:T(8,128)S(1)}, f32[1,256,1024]{2,1,0:T(8,128)S(1)}) custom-call(bf16[128,1024]{1,0:T(8,128)(2,1)S(1)} %copy-done.2, bf16[128,1024]{1,0:T(8,128)(2,1)S(1)} %copy-done.3, s32[2,128]{1,0:T(2,128)S(1)} %bitcast.2, f32[2,128]{1,0:T(2,128)S(1)} %bitcast.3, ...), custom_call_target="tpu_custom_call" | custom-call | tf_op jit(solution)/shard_map/pallas_call | solution.py:424
  91.4 0.0 copy-start
  91.4 1.0 copy-done
  92.4 0.0 copy-start.1
  92.4 1.0 %copy-done.1 = f32[1,256,1024]{2,1,0:T(8,128)} copy-done((f32[1,256,1024]{2,1,0:T(8,128)}, f32[1,256,1024]{2,1,0:T(8,128)S(1)}, u32[]{:S(2)}) %copy-start.1) | copy-done | bytes 1048600
  93.4 0.0 copy-start.4
  93.4 0.7 copy-done.4
  94.1 0.0 copy-start.5
  94.1 0.7 copy-done.5
  94.8 3.2 %shard_map.94 = (bf16[128,1024]{1,0:T(8,128)(2,1)}, bf16[128,1024]{1,0:T(8,128)(2,1)}, f32[1,128,2048]{2,1,0:T(8,128)}, f32[1,256,1024]{2,1,0:T(8,128)}) custom-call(bf16[128,1024]{1,0:T(8,128)(2,1)} %copy-done.4, bf16[128,1024]{1,0:T(8,128)(2,1)} %copy-done.5, f32[1,128,2048]{2,1,0:T(8,128)} %copy-done, f32[1,256,1024]{2,1,0:T(8,128)} %copy-done.1), custom_call_target="tpu_custom_call" | custom-call | tf_op jit(solution)/shard_map/pallas_call | solution.py:478
Async XLA Ops:
  0.6 1.0 copy-start.2
  1.6 0.9 copy-start.3
  2.5 0.7 copy-start.6
  3.2 0.7 copy-start.7
  91.4 1.0 copy-start
  92.4 1.0 %copy-start.1 = (f32[1,256,1024]{2,1,0:T(8,128)}, f32[1,256,1024]{2,1,0:T(8,128)S(1)}, u32[]{:S(2)}) copy-start(f32[1,256,1024]{2,1,0:T(8,128)S(1)} %get-tuple-element.11.refs_3_) | copy-start | bytes 3145732
  93.4 0.7 copy-start.4
  94.1 0.7 copy-start.5

commit v4 on v3

--- a/solution.py
+++ b/solution.py
@@ -293,15 +293,19 @@
 
     to_y, to_z = {}, {}
 
-    def send_y(kind, dz):
+    def ready_y(kind, dz):
         total = sums[kind][1, dz] + term(kind, dz, 1, late)
         (syi, syo)[kind][dz] = total.astype(jnp.bfloat16)
-        for n in (2 * kind, 2 * kind + 1):
-            src, at = split(n, (syi, syo))
-            dst, _ = split(n, (ryi, ryo))
-            to_y[n, dz] = push(
-                src.at[dz, at], dst.at[dz, at], y_send.at[dz, n], y_recv.at[dz, n], at_y
-            )
+
+    order_y = [(n, dz) for dz in (1, 0) for n in range(4)]
+
+    def next_y():
+        n, dz = order_y[len(to_y)]
+        if to_y:
+            to_y[order_y[len(to_y) - 1]].wait_send()
+        src, at = split(n, (syi, syo))
+        dst, _ = split(n, (ryi, ryo))
+        to_y[n, dz] = push(src.at[dz, at], dst.at[dz, at], y_send.at[dz, n], y_recv.at[dz, n], at_y)
 
     def over_y(n, dz):
         own, at = split(n, sums)
@@ -341,42 +345,50 @@
     wait_slot(7)
     hidden_pair(3)
 
-    for kind in range(2):
-        send_y(kind, 1)
+    ready_y(0, 1)
+    next_y()
+    ready_y(1, 1)
     for kind in range(2):
         keep(kind, 1)
     back_and_give(3)
+    next_y()
     send_z(0)
-    back_and_give(2)
     take(0, by_core[0, 3], 3, 6)
     x_m2 = give(0, 6, 5, at_x)
     take(1, by_core[1, 3], 3, 6)
     z_g4 = give(1, 6, 5, at_zlo)
-    send_z(1)
-    send_y(0, 0)
-    back_and_give(1)
+    back_and_give(2)
     take(0, by_core[0, 2], 2, 4)
     x_m0 = give(0, 4, 4, at_x)
-    send_z(2)
-    send_y(1, 0)
+    next_y()
+    send_z(1)
+    back_and_give(1)
     take(1, by_core[1, 1], 1, 2)
     z_g0 = give(1, 2, 4, at_zlo)
-    send_z(3)
+    ready_y(0, 0)
+    ready_y(1, 0)
+    next_y()
+    send_z(2)
     take(1, by_core[1, 2], 2, 4)
     take(0, by_core[0, 1], 1, 2)
     take(0, by_core[0, 0], 0, 0)
     take(1, by_core[1, 0], 0, 0)
+    for kind in range(2):
+        keep(kind, 0)
+    next_y()
+    send_z(3)
     take(0, x_m2, 5, 2)
     z_m0 = give(0, 2, 6, at_zlo)
     take(1, z_g4, 5, 4)
     x_g0 = give(1, 4, 6, at_x)
-    for kind in range(2):
-        keep(kind, 0)
+    next_y()
     take(0, x_m0, 4, 0)
     take(1, z_g0, 4, 0)
+    next_y()
 
     sl[...] = finish(0).astype(jnp.bfloat16)
     last = push(sl, rl, l_send, l_recv, at_zlo)
+    next_y()
 
     z_m0.wait_recv()
     x_g0.wait_recv()
@@ -399,14 +411,24 @@
         where = pl.ds(pl.multiple_of(run * half + (1 - zlo) * chunk, 128), chunk)
         grad_w_in[0, :, where] = rl[:, run * chunk : (run + 1) * chunk].astype(jnp.float32)
     grad_w_out[0, h_part:] = finish(3)
+    waited = [to_y[key] for key in order_y[:-1]]
     for copy in sent:
-        copy.wait_send()
+        if not any(copy is other for other in waited):
+            copy.wait_send()
 
 
 def hand_on(*refs):
-    count = len(refs) // 2
-    for source, target in zip(refs[:count], refs[count:]):
-        target[...] = source[...]
+    count = (len(refs) - 1) // 3
+    sources, targets, held, sems = refs[:count], refs[count : 2 * count], refs[2 * count : -1], refs[-1]
+    loads = [pltpu.make_async_copy(a, h, sems.at[0, i]) for i, (a, h) in enumerate(zip(sources, held))]
+    stores = [pltpu.make_async_copy(h, b, sems.at[1, i]) for i, (h, b) in enumerate(zip(held, targets))]
+    for load in loads:
+        load.start()
+    for load, store in zip(loads, stores):
+        load.wait()
+        store.start()
+    for store in stores:
+        store.wait()
 
 
 def fused(frames, expert_ids, gate_weights, cotangent, w_in, w_out):
@@ -470,7 +492,7 @@
                 dma(()),
             ],
             compiler_params=pltpu.CompilerParams(
-                collective_id=0, has_side_effects=True, vmem_limit_bytes=48 * 2**20
+                collective_id=0, has_side_effects=True, vmem_limit_bytes=60 * 2**20
             ),
         )(frames, cotangent, expert_ids.T, gate_weights.T, w_in, w_out)
     )
@@ -478,8 +500,10 @@
         pl.pallas_call(
             hand_on,
             out_shape=tuple(jax.ShapeDtypeStruct(r.shape, r.dtype) for r in results),
-            in_specs=[in_vmem] * 4,
-            out_specs=(in_vmem,) * 4,
+            in_specs=[anywhere] * 4,
+            out_specs=(anywhere,) * 4,
+            scratch_shapes=[vmem(r.shape, r.dtype) for r in results] + [dma((2, 4))],
+            compiler_params=pltpu.CompilerParams(vmem_limit_bytes=60 * 2**20),
         )(*results)
     )
 

time: 98.3 us -> 91.8 us (0.934)
  local copies, waits for them, and re-layouts: 6.64 us -> 0 us
    unnamed x16 -> x0, local copies, waits for them, and re-layouts: 6.64 us -> none
where the time goes in v4:
time: 91.8 us; the launch traced here: 91.6 us
  Pallas kernels  91 us (99%)
    pallas_call x1, Pallas kernels, fused(): pl.pallas_call(functools.partial(layer_kernel, min(256, half)), out_shape...  88.2 us
    pallas_call x1, Pallas kernels, fused(): pl.pallas_call(hand_on, out_shape=tuple((jax.ShapeDtypeStruct(r.shape, r....  2.78 us

profile of v4, /device:TPU:0, one launch (start us, length us, event | category | flops | bytes accessed | tf_op | source)
XLA Modules:
  0.0 91.6 jit_solution(17500086182982310299)
XLA Ops:
  0.6 88.2 %shard_map.93 = (bf16[128,1024]{1,0:T(8,128)(2,1)}, bf16[128,1024]{1,0:T(8,128)(2,1)}, f32[1,128,2048]{2,1,0:T(8,128)}, f32[1,256,1024]{2,1,0:T(8,128)}) custom-call(bf16[128,1024]{1,0:T(8,128)(2,1)} %frames.1, bf16[128,1024]{1,0:T(8,128)(2,1)} %cot.1, s32[2,128]{1,0:T(2,128)} %bitcast.2, f32[2,128]{1,0:T(2,128)} %bitcast.3, bf16[1,1024,2048]{2,1,0:T(8,128)(2,1)} %w_in.1, ...), custom_call_target="tpu_custom_call" | custom-call | tf_op jit(solution)/shard_map/pallas_call | solution.py:446
  88.9 2.8 %shard_map.94 = (bf16[128,1024]{1,0:T(8,128)(2,1)}, bf16[128,1024]{1,0:T(8,128)(2,1)}, f32[1,128,2048]{2,1,0:T(8,128)}, f32[1,256,1024]{2,1,0:T(8,128)}) custom-call(bf16[128,1024]{1,0:T(8,128)(2,1)} %get-tuple-element.8.refs_0_, bf16[128,1024]{1,0:T(8,128)(2,1)} %get-tuple-element.9.refs_1_, f32[1,128,2048]{2,1,0:T(8,128)} %get-tuple-element.10.refs_2_, ...), custom_call_target="tpu_custom_call" | custom-call | tf_op jit(solution)/shard_map/pallas_call | solution.py:500

commit v5 on v4

--- a/solution.py
+++ b/solution.py
@@ -143,22 +143,21 @@
     zlo, y = lax.div(rest, 2), lax.rem(rest, 2)
     x, core = lax.div(e, 2), lax.rem(e, 2)
     at_y = (d + 1 - 2 * y, e)
-    at_zlo = (d + 2 - 4 * zlo, e)
-    at_zhi = (d + 4 - 8 * zhi, e)
+    at_near = (d + 2 - 4 * zlo, e)
+    at_far = (d + 4 - 8 * zhi, e)
     at_core = (d, e + 1 - 2 * core)
     at_x = (d, e + 2 - 4 * x)
 
-    loads = []
-    for run in range(2):
-        where = pl.ds(pl.multiple_of(run * half + zlo * chunk, 128), chunk)
-        here = pl.ds(run * chunk, chunk)
-        loads.append(pltpu.make_async_copy(w_in.at[0, :, where], wi.at[:, here], w_sem.at[2 * run]))
-        loads.append(pltpu.make_async_copy(w_out.at[0, where, :], wo.at[here, :], w_sem.at[2 * run + 1]))
+    half_at = pl.ds(pl.multiple_of(zhi * half, 128), half)
+    loads = [
+        pltpu.make_async_copy(w_in.at[0, :, half_at], wi, w_sem.at[0]),
+        pltpu.make_async_copy(w_out.at[0, half_at, :], wo, w_sem.at[1]),
+    ]
     for load in loads:
         load.start()
 
     barrier = pltpu.get_barrier_semaphore()
-    for peer in (at_y, at_zlo, at_zhi, at_core, at_x):
+    for peer in (at_y, at_near, at_far, at_core, at_x):
         pl.semaphore_signal(barrier, inc=1, device_id=peer, device_id_type=MESH)
 
     def slot(s, count=1):
@@ -200,12 +199,7 @@
     )
     nrm[slot(0)] = standardize(frames[...].astype(jnp.float32))[0].astype(jnp.bfloat16)
     pl.semaphore_wait(barrier, 5)
-    forward((0,), 0, ((2, at_zlo),))
-    forward((1,), 0, ((4, at_x),))
-    forward((2,), 0, ((2, at_zlo), (4, at_x), (1, at_core)))
-    forward((0, 1), 0, ((1, at_core),))
-    forward((1,), 0, ((2, at_zlo),))
-    forward((0,), 0, ((4, at_x),))
+    forward((2, 0, 1), 0, ((2, at_far), (1, at_core), (4, at_x)))
     for load in loads:
         load.wait()
 
@@ -268,15 +262,15 @@
     early, late = slot(0, blocks - 2), slot(blocks - 2, 2)
 
     def term(kind, dz, dy, some):
-        zh = zhi if dz == 0 else 1 - zhi
+        near = zlo if dz == 0 else 1 - zlo
         yy = y if dy == 0 else 1 - y
         if kind == 0:
             parts = [
-                nrm[some, pl.ds(pl.multiple_of((4 * zh + 2 * zl + yy) * d_own, 128), d_own)]
-                for zl in (1 - zlo, zlo)
+                nrm[some, pl.ds(pl.multiple_of((4 * far + 2 * near + yy) * d_own, 128), d_own)]
+                for far in (1 - zhi, zhi)
             ]
             return dot(jnp.concatenate(parts, axis=1), gpre[some], 0, 0)
-        part = pl.ds(pl.multiple_of(zh * chunk + yy * h_own, 128), h_own)
+        part = pl.ds(pl.multiple_of(near * chunk + yy * h_own, 128), h_own)
         return dot(hid[some, part], grow[some], 0, 0)
 
     sums = (owi, owo)
@@ -284,54 +278,53 @@
     def begin(kind, dz, dy):
         sums[kind][dy, dz] = term(kind, dz, dy, early)
 
-    def keep(kind, dz):
-        sums[kind][0, dz] = sums[kind][0, dz] + term(kind, dz, 0, late)
+    def total(kind, dz, dy):
+        sums[kind][dy, dz] = sums[kind][dy, dz] + term(kind, dz, dy, late)
 
     def split(n, buffers):
         rows_of = d_own if n < 2 else h_part
         return buffers[n // 2], pl.ds(n % 2 * rows_of, rows_of)
 
-    to_y, to_z = {}, {}
-
-    def ready_y(kind, dz):
-        total = sums[kind][1, dz] + term(kind, dz, 1, late)
-        (syi, syo)[kind][dz] = total.astype(jnp.bfloat16)
-
-    order_y = [(n, dz) for dz in (1, 0) for n in range(4)]
-
-    def next_y():
-        n, dz = order_y[len(to_y)]
-        if to_y:
-            to_y[order_y[len(to_y) - 1]].wait_send()
+    one, two = {}, {}
+
+    def place_of(n, first, second):
+        return (second, first) if n == 0 else (first, second)
+
+    def first_step(n, bit):
         src, at = split(n, (syi, syo))
         dst, _ = split(n, (ryi, ryo))
-        to_y[n, dz] = push(src.at[dz, at], dst.at[dz, at], y_send.at[dz, n], y_recv.at[dz, n], at_y)
-
-    def over_y(n, dz):
-        own, at = split(n, sums)
-        got, _ = split(n, (ryi, ryo))
-        to_y[n, dz].wait_recv()
-        return own[0, dz, at] + got[dz, at].astype(jnp.float32)
-
-    def send_z(n):
+        dy, dz = place_of(n, 1, bit)
+        src[bit, at] = sums[n // 2][dy, dz, at].astype(jnp.bfloat16)
+        one[n, bit] = push(
+            src.at[bit, at], dst.at[bit, at], y_send.at[bit, n], y_recv.at[bit, n],
+            at_y if n else at_near,
+        )
+
+    def after_first(n, bit):
+        got, at = split(n, (ryi, ryo))
+        dy, dz = place_of(n, 0, bit)
+        one[n, bit].wait_recv()
+        return sums[n // 2][dy, dz, at] + got[bit, at].astype(jnp.float32)
+
+    def second_step(n):
         src, at = split(n, (szi, szo))
         dst, _ = split(n, (rzi, rzo))
-        src[at] = over_y(n, 1).astype(jnp.bfloat16)
-        to_z[n] = push(src.at[at], dst.at[at], z_send.at[n], z_recv.at[n], at_zhi)
+        src[at] = after_first(n, 1).astype(jnp.bfloat16)
+        two[n] = push(
+            src.at[at], dst.at[at], z_send.at[n], z_recv.at[n], at_near if n else at_y
+        )
 
     def finish(n):
         got, at = split(n, (rzi, rzo))
-        total = over_y(n, 0)
-        to_z[n].wait_recv()
-        return total + got[at].astype(jnp.float32)
+        result = after_first(n, 0)
+        two[n].wait_recv()
+        return result + got[at].astype(jnp.float32)
 
     wait_slot(1)
     hidden_pair(0)
     back_and_give(0)
-    forward((2, 0), 2, ((6, at_x), (3, at_core)))
-    forward((1,), 4, ((6, at_zlo), (5, at_core)))
-    forward((1,), 2, ((3, at_core),))
-    forward((2, 0), 4, ((5, at_core),))
+    forward((2, 0, 1), 2, ((6, at_x), (3, at_core)))
+    forward((2, 0, 1), 4, ((5, at_core),))
     wait_slot(3)
     hidden_pair(1)
     wait_slot(5)
@@ -345,76 +338,66 @@
     wait_slot(7)
     hidden_pair(3)
 
-    ready_y(0, 1)
-    next_y()
-    ready_y(1, 1)
+    total(0, 1, 1)
+    first_step(0, 1)
+    first_step(1, 1)
+    total(1, 1, 1)
+    first_step(2, 1)
+    first_step(3, 1)
+    total(0, 1, 0)
+    first_step(0, 0)
+    total(0, 0, 1)
+    back_and_give(3)
+    second_step(0)
+    second_step(1)
+    first_step(1, 0)
+    for k in range(2):
+        take(k, by_core[k, 3], 3, 6)
+    by_x = {(k, 2): give(k, 6, 5, at_x) for k in range(2)}
+    back_and_give(2)
+    total(1, 1, 0)
+    total(1, 0, 1)
+    second_step(2)
+    first_step(2, 0)
+    first_step(3, 0)
+    for k in range(2):
+        take(k, by_core[k, 2], 2, 4)
+    for k in range(2):
+        by_x[k, 0] = give(k, 4, 4, at_x)
+    back_and_give(1)
+    second_step(3)
+    for k in range(2):
+        take(k, by_core[k, 1], 1, 2)
+        take(k, by_core[k, 0], 0, 0)
     for kind in range(2):
-        keep(kind, 1)
-    back_and_give(3)
-    next_y()
-    send_z(0)
-    take(0, by_core[0, 3], 3, 6)
-    x_m2 = give(0, 6, 5, at_x)
-    take(1, by_core[1, 3], 3, 6)
-    z_g4 = give(1, 6, 5, at_zlo)
-    back_and_give(2)
-    take(0, by_core[0, 2], 2, 4)
-    x_m0 = give(0, 4, 4, at_x)
-    next_y()
-    send_z(1)
-    back_and_give(1)
-    take(1, by_core[1, 1], 1, 2)
-    z_g0 = give(1, 2, 4, at_zlo)
-    ready_y(0, 0)
-    ready_y(1, 0)
-    next_y()
-    send_z(2)
-    take(1, by_core[1, 2], 2, 4)
-    take(0, by_core[0, 1], 1, 2)
-    take(0, by_core[0, 0], 0, 0)
-    take(1, by_core[1, 0], 0, 0)
-    for kind in range(2):
-        keep(kind, 0)
-    next_y()
-    send_z(3)
-    take(0, x_m2, 5, 2)
-    z_m0 = give(0, 2, 6, at_zlo)
-    take(1, z_g4, 5, 4)
-    x_g0 = give(1, 4, 6, at_x)
-    next_y()
-    take(0, x_m0, 4, 0)
-    take(1, z_g0, 4, 0)
-    next_y()
+        total(kind, 0, 0)
+    by_far = []
+    for k in range(2):
+        take(k, by_x[k, 2], 5, 2)
+        by_far.append(give(k, 2, 6, at_far))
 
     sl[...] = finish(0).astype(jnp.bfloat16)
-    last = push(sl, rl, l_send, l_recv, at_zlo)
-    next_y()
-
-    z_m0.wait_recv()
-    x_g0.wait_recv()
+    last = push(sl, rl, l_send, l_recv, at_far)
+    for k in range(2):
+        take(k, by_x[k, 0], 4, 0)
+    for copy in by_far:
+        copy.wait_recv()
     values = frames[...].astype(jnp.float32)
-    total = pm[slot(0)].astype(jnp.float32) + rm[slot(6)].astype(jnp.float32)
-    mixed[...] = (values + total).astype(jnp.bfloat16)
+    added = pm[slot(0)].astype(jnp.float32) + rm[slot(6)].astype(jnp.float32)
+    mixed[...] = (values + added).astype(jnp.bfloat16)
     standardized, inverse = standardize(values)
     grad = pg[slot(0)].astype(jnp.float32) + rg[slot(6)].astype(jnp.float32)
     centered = grad - jnp.mean(grad, axis=-1, keepdims=True)
     along = standardized * jnp.mean(grad * standardized, axis=-1, keepdims=True)
     grad_frames[...] = (cot[...].astype(jnp.float32) + inverse * (centered - along)).astype(jnp.bfloat16)
 
-    final = finish(1)
-    for run in range(2):
-        where = pl.ds(pl.multiple_of(run * half + zlo * chunk, 128), chunk)
-        grad_w_in[0, :, where] = final[:, run * chunk : (run + 1) * chunk]
+    grad_w_in[0, :, half_at] = finish(1)
     grad_w_out[0, :h_part] = finish(2)
     last.wait_recv()
-    for run in range(2):
-        where = pl.ds(pl.multiple_of(run * half + (1 - zlo) * chunk, 128), chunk)
-        grad_w_in[0, :, where] = rl[:, run * chunk : (run + 1) * chunk].astype(jnp.float32)
+    grad_w_in[0, :, pl.ds(pl.multiple_of((1 - zhi) * half, 128), half)] = rl[...].astype(jnp.float32)
     grad_w_out[0, h_part:] = finish(3)
-    waited = [to_y[key] for key in order_y[:-1]]
     for copy in sent:
-        if not any(copy is other for other in waited):
-            copy.wait_send()
+        copy.wait_send()
 
 
 def hand_on(*refs):
@@ -479,7 +462,7 @@
                 vmem((2 * d_own, half), bf),
                 vmem((d_own, half), bf),
                 vmem((d_own, half), bf),
-                dma((4,)),
+                dma((2,)),
                 dma((3, blocks)),
                 dma((3, blocks)),
                 dma((2, 7)),

time: 91.8 us -> 101 us (1.10)
  Pallas kernels: 91 us -> 99.9 us
    pallas_call x1, Pallas kernels: 88.2 us -> 97.2 us  [fused(): pl.pallas_call(functools.partial(layer_kernel, min(256, half)), out_shape...]
where the time goes in v5:
time: 101 us
  Pallas kernels  99.9 us (99%)
    pallas_call x1, Pallas kernels, fused(): pl.pallas_call(functools.partial(layer_kernel, min(256, half)), out_shape...  97.2 us
    pallas_call x1, Pallas kernels, fused(): pl.pallas_call(hand_on, out_shape=tuple((jax.ShapeDtypeStruct(r.shape, r....  2.78 us

profile of v5, /device:TPU:0, one launch (start us, length us, event | category | flops | bytes accessed | tf_op | source)
XLA Modules:
  0.0 100.6 jit_solution(5951792269953417365)
XLA Ops:
  0.6 97.2 %shard_map.93 = (bf16[128,1024]{1,0:T(8,128)(2,1)}, bf16[128,1024]{1,0:T(8,128)(2,1)}, f32[1,128,2048]{2,1,0:T(8,128)}, f32[1,256,1024]{2,1,0:T(8,128)}) custom-call(bf16[128,1024]{1,0:T(8,128)(2,1)} %frames.1, bf16[128,1024]{1,0:T(8,128)(2,1)} %cot.1, s32[2,128]{1,0:T(2,128)} %bitcast.2, f32[2,128]{1,0:T(2,128)} %bitcast.3, bf16[1,1024,2048]{2,1,0:T(8,128)(2,1)} %w_in.1, ...), custom_call_target="tpu_custom_call" | custom-call | tf_op jit(solution)/shard_map/pallas_call | solution.py:429
  97.8 2.8 %shard_map.94 = (bf16[128,1024]{1,0:T(8,128)(2,1)}, bf16[128,1024]{1,0:T(8,128)(2,1)}, f32[1,128,2048]{2,1,0:T(8,128)}, f32[1,256,1024]{2,1,0:T(8,128)}) custom-call(bf16[128,1024]{1,0:T(8,128)(2,1)} %get-tuple-element.8.refs_0_, bf16[128,1024]{1,0:T(8,128)(2,1)} %get-tuple-element.9.refs_1_, f32[1,128,2048]{2,1,0:T(8,128)} %get-tuple-element.10.refs_2_, ...), custom_call_target="tpu_custom_call" | custom-call | tf_op jit(solution)/shard_map/pallas_call | solution.py:483

commit v6 on v4

--- a/solution.py
+++ b/solution.py
@@ -301,8 +301,6 @@
 
     def next_y():
         n, dz = order_y[len(to_y)]
-        if to_y:
-            to_y[order_y[len(to_y) - 1]].wait_send()
         src, at = split(n, (syi, syo))
         dst, _ = split(n, (ryi, ryo))
         to_y[n, dz] = push(src.at[dz, at], dst.at[dz, at], y_send.at[dz, n], y_recv.at[dz, n], at_y)
@@ -345,50 +343,48 @@
     wait_slot(7)
     hidden_pair(3)
 
-    ready_y(0, 1)
-    next_y()
-    ready_y(1, 1)
     for kind in range(2):
-        keep(kind, 1)
+        ready_y(kind, 1)
+        next_y()
+        next_y()
+    keep(0, 1)
     back_and_give(3)
-    next_y()
-    send_z(0)
     take(0, by_core[0, 3], 3, 6)
     x_m2 = give(0, 6, 5, at_x)
     take(1, by_core[1, 3], 3, 6)
     z_g4 = give(1, 6, 5, at_zlo)
+    send_z(0)
+    keep(1, 1)
+    ready_y(0, 0)
+    next_y()
+    next_y()
+    send_z(1)
     back_and_give(2)
     take(0, by_core[0, 2], 2, 4)
     x_m0 = give(0, 4, 4, at_x)
+    ready_y(1, 0)
     next_y()
-    send_z(1)
+    next_y()
+    send_z(2)
     back_and_give(1)
     take(1, by_core[1, 1], 1, 2)
     z_g0 = give(1, 2, 4, at_zlo)
-    ready_y(0, 0)
-    ready_y(1, 0)
-    next_y()
-    send_z(2)
+    send_z(3)
     take(1, by_core[1, 2], 2, 4)
     take(0, by_core[0, 1], 1, 2)
     take(0, by_core[0, 0], 0, 0)
     take(1, by_core[1, 0], 0, 0)
     for kind in range(2):
         keep(kind, 0)
-    next_y()
-    send_z(3)
     take(0, x_m2, 5, 2)
     z_m0 = give(0, 2, 6, at_zlo)
     take(1, z_g4, 5, 4)
     x_g0 = give(1, 4, 6, at_x)
-    next_y()
     take(0, x_m0, 4, 0)
     take(1, z_g0, 4, 0)
-    next_y()
 
     sl[...] = finish(0).astype(jnp.bfloat16)
     last = push(sl, rl, l_send, l_recv, at_zlo)
-    next_y()
 
     z_m0.wait_recv()
     x_g0.wait_recv()
@@ -411,10 +407,8 @@
         where = pl.ds(pl.multiple_of(run * half + (1 - zlo) * chunk, 128), chunk)
         grad_w_in[0, :, where] = rl[:, run * chunk : (run + 1) * chunk].astype(jnp.float32)
     grad_w_out[0, h_part:] = finish(3)
-    waited = [to_y[key] for key in order_y[:-1]]
     for copy in sent:
-        if not any(copy is other for other in waited):
-            copy.wait_send()
+        copy.wait_send()
 
 
 def hand_on(*refs):

time: 91.8 us -> 99 us (1.078)
  Pallas kernels: 91 us -> 98.2 us
    pallas_call x1, Pallas kernels: 88.2 us -> 95.5 us  [fused(): pl.pallas_call(functools.partial(layer_kernel, min(256, half)), out_shape...]
where the time goes in v6:
time: 99 us; the launch traced here: 98.9 us
  Pallas kernels  98.2 us (99%)
    pallas_call x1, Pallas kernels, fused(): pl.pallas_call(functools.partial(layer_kernel, min(256, half)), out_shape...  95.5 us
    pallas_call x1, Pallas kernels, fused(): pl.pallas_call(hand_on, out_shape=tuple((jax.ShapeDtypeStruct(r.shape, r....  2.78 us

profile of v6, /device:TPU:0, one launch (start us, length us, event | category | flops | bytes accessed | tf_op | source)
XLA Modules:
  0.0 98.9 jit_solution(7773525454774368426)
XLA Ops:
  0.6 95.5 %shard_map.93 = (bf16[128,1024]{1,0:T(8,128)(2,1)}, bf16[128,1024]{1,0:T(8,128)(2,1)}, f32[1,128,2048]{2,1,0:T(8,128)}, f32[1,256,1024]{2,1,0:T(8,128)}) custom-call(bf16[128,1024]{1,0:T(8,128)(2,1)} %frames.1, bf16[128,1024]{1,0:T(8,128)(2,1)} %cot.1, s32[2,128]{1,0:T(2,128)} %bitcast.2, f32[2,128]{1,0:T(2,128)} %bitcast.3, bf16[1,1024,2048]{2,1,0:T(8,128)(2,1)} %w_in.1, ...), custom_call_target="tpu_custom_call" | custom-call | tf_op jit(solution)/shard_map/pallas_call | solution.py:440
  96.1 2.8 %shard_map.94 = (bf16[128,1024]{1,0:T(8,128)(2,1)}, bf16[128,1024]{1,0:T(8,128)(2,1)}, f32[1,128,2048]{2,1,0:T(8,128)}, f32[1,256,1024]{2,1,0:T(8,128)}) custom-call(bf16[128,1024]{1,0:T(8,128)(2,1)} %get-tuple-element.8.refs_0_, bf16[128,1024]{1,0:T(8,128)(2,1)} %get-tuple-element.9.refs_1_, f32[1,128,2048]{2,1,0:T(8,128)} %get-tuple-element.10.refs_2_, ...), custom_call_target="tpu_custom_call" | custom-call | tf_op jit(solution)/shard_map/pallas_call | solution.py:494
